TPU v7x, 512 devices: a whole 4x8x8 slice. The times are simulated.
512 devices in a mesh: strike: 8 (over x, core), dev: 64 (over z, y).
Axes of the slice: x: 4, y: 8, z: 8, core: 2. Of those that a mesh axis runs over, the one named last changes fastest.
Arguments:
- log_rate: float32 [32, 1024, 256], P(None, ('strike', 'dev')), may hold values from -1.5 to 1.5
- state_log: float32 [32, 1024, 256], P(None, ('strike', 'dev')), may hold values from -1 to 1
- a_coef: float32 [1024, 256], P(('strike', 'dev')), may hold values from 0.5 to 2
- b_coef: float32 [1024, 256], P(('strike', 'dev')), may hold values from 0.5 to 2
- near_src: int32 [512, 32], P(('strike', 'dev')), may hold values from 0 to 127, as said below
- near_dst: int32 [512, 32], P(('strike', 'dev')), may hold values from 0 to 1
- near_count: int32 [512], P(('strike', 'dev')), may hold values from 8 to 32, as said below
- near_blocks: bfloat16 [512, 32, 256, 256], P(('strike', 'dev')), may hold values from -0.1875 to 0.1875
- far_src: int32 [512, 32], P(('strike', 'dev')), may hold values from 0 to 127
- far_dst: int32 [512, 32], P(('strike', 'dev')), may hold values from 0 to 1
- far_coupling: float32 [512, 32, 32, 32], P(('strike', 'dev')), may hold values from -1 to 1
- cluster_bases: bfloat16 [1024, 32, 256], P(('strike', 'dev')), may hold values from -0.375 to 0.375
- transfer: float32 [1024, 32, 32], P(('strike', 'dev')), may hold values from -0.1875 to 0.1875
- coarse_coupling: float32 [1024, 8, 32, 32], P(('strike', 'dev')), may hold values from -0.625 to 0.625
Outputs:
- new_rate: float32 [32, 1024, 256], P(None, ('strike', 'dev'))
- new_state: float32 [32, 1024, 256], P(None, ('strike', 'dev'))
Inputs may be any that keep to these rules, and one draw needn't show every extreme that they name: `near_src`: each near source cluster is owned by a device of the same strike group whose dev index differs from the holder's by at most 2. Only a device's first near_count slots are live; some device has all 32 slots live.
All inputs are finite; a program needn't handle non-finite values.
Results may differ from a plain program's by a relative error of at most 0.0045.
Values may be sent and summed in bfloat16 or wider, within the bound.
A program may use at most 64 MiB of HBM per device.

v0:
```python
import jax
import jax.numpy as jnp
from jax import lax
from jax.sharding import PartitionSpec as P

CL = 2
NB = 32
REACH = 2


time_step = 0.25
viscous = 0.5
highest = lax.Precision.HIGHEST


def from_behind(block, axis, distance):
    devices = range(lax.axis_size(axis))
    route = [(i - distance, i) for i in devices if i - distance in devices]
    return lax.ppermute(block, axis, route)


def near_field(deficit, sources, targets, live_count, blocks):
    pieces = []
    for offset in range(-REACH, REACH + 1):
        if offset == 0:
            pieces.append(deficit)
        else:
            pieces.append(from_behind(deficit, "dev", -offset))
    rate_table = jnp.concatenate(pieces, axis=1)
    own_dev = lax.axis_index("dev")
    slot_of = (sources // CL - own_dev + REACH) * CL + sources % CL
    src_rows = jnp.take(rate_table, slot_of, axis=1)
    products = jnp.einsum("ekp,kpq->ekq", src_rows, blocks, preferred_element_type=jnp.float32)
    live_mask = (jnp.arange(NB, dtype=jnp.int32) < live_count).astype(jnp.float32)
    receiver_pick = (targets[:, None] == jnp.arange(CL, dtype=jnp.int32)[None, :]).astype(
        jnp.float32
    ) * live_mask[:, None]
    return jnp.einsum("ekq,kc->ecq", products, receiver_pick, precision=highest)


def slopes(
    rate_log,
    state_now,
    a_coef,
    b_coef,
    sources,
    targets,
    live_count,
    blocks,
    far_src,
    far_dst,
    far_coupling,
    cluster_bases,
    transfer,
    coarse_coupling,
):
    velocity = jnp.exp(rate_log)
    deficit = (velocity - 1.0).astype(jnp.bfloat16)
    near = near_field(deficit, sources, targets, live_count, blocks)
    coefs = jnp.einsum("ecp,crp->ecr", deficit, cluster_bases, preferred_element_type=jnp.float32)
    group_part = jnp.einsum("ecr,crs->es", coefs, transfer, precision=highest)
    all_coefs = lax.all_gather(coefs, "dev", axis=1, tiled=True)
    group_total = lax.psum(group_part, "dev")
    all_groups = lax.all_gather(group_total[None], "strike", axis=0, tiled=True)
    src_coefs = jnp.take(all_coefs, far_src, axis=1)
    far_terms = jnp.einsum("ekr,krs->eks", src_coefs, far_coupling, precision=highest)
    far_pick = (far_dst[:, None] == jnp.arange(CL, dtype=jnp.int32)[None, :]).astype(jnp.float32)
    far_part = jnp.einsum("eks,kc->ecs", far_terms, far_pick, precision=highest)
    coarse = jnp.einsum("her,chrs->ecs", all_groups, coarse_coupling, precision=highest)
    expansion = (far_part + coarse).astype(jnp.bfloat16)
    far = jnp.einsum("ecr,crp->ecp", expansion, cluster_bases, preferred_element_type=jnp.float32)
    stress_rate = -(near + far)
    state_change = jnp.exp(-state_now) - velocity
    rate_change = (stress_rate - b_coef[None] * state_change) / (a_coef[None] + viscous * velocity)
    return (rate_change, state_change)


def per_device(
    log_rate,
    state_log,
    a_coef,
    b_coef,
    near_src,
    near_dst,
    near_count,
    near_blocks,
    far_src,
    far_dst,
    far_coupling,
    cluster_bases,
    transfer,
    coarse_coupling,
):

    def slope_at(rate_log, state_now):
        return slopes(
            rate_log,
            state_now,
            a_coef,
            b_coef,
            near_src[0],
            near_dst[0],
            near_count[0],
            near_blocks[0],
            far_src[0],
            far_dst[0],
            far_coupling[0],
            cluster_bases,
            transfer,
            coarse_coupling,
        )

    first = slope_at(log_rate, state_log)
    second = slope_at(log_rate + 0.5 * time_step * first[0], state_log + 0.5 * time_step * first[1])
    third = slope_at(
        log_rate + 0.5 * time_step * second[0], state_log + 0.5 * time_step * second[1]
    )
    fourth = slope_at(log_rate + time_step * third[0], state_log + time_step * third[1])
    new_rate = log_rate + time_step / 6.0 * (
        first[0] + 2.0 * second[0] + 2.0 * third[0] + fourth[0]
    )
    new_state = state_log + time_step / 6.0 * (
        first[1] + 2.0 * second[1] + 2.0 * third[1] + fourth[1]
    )
    return (new_rate, new_state)


def solution(mesh):
    placed = (
        P(None, ("strike", "dev"), None),
        P(None, ("strike", "dev"), None),
        P(("strike", "dev"), None),
        P(("strike", "dev"), None),
        P(("strike", "dev"), None),
        P(("strike", "dev"), None),
        P(("strike", "dev")),
        P(("strike", "dev"), None, None, None),
        P(("strike", "dev"), None),
        P(("strike", "dev"), None),
        P(("strike", "dev"), None, None, None),
        P(("strike", "dev"), None, None),
        P(("strike", "dev"), None, None),
        P(("strike", "dev"), None, None, None),
    )
    return jax.shard_map(
        per_device,
        mesh=mesh,
        in_specs=placed,
        out_specs=(P(None, ("strike", "dev"), None), P(None, ("strike", "dev"), None)),
        check_vma=False,
    )
```

profile of v0, /device:TPU:1, one launch (start us, length us, event | category | flops | bytes accessed | tf_op | source)
XLA Modules:
  0.0 1487.1 jit_solution(8770723316534152707)
XLA Ops:
  0.7 1.5 add_convert_fusion.3
  2.2 5.6 collective-permute-start
  7.8 3.8 collective-permute-start.1
  11.6 1.3 collective-permute-start.2
  12.9 1.3 collective-permute-start.3
  14.9 1.2 compare_and_fusion
  17.5 0.9 convolution_bitcast_fusion.7
  18.4 50.2 %all_gather.24 = f32[32,128,32]{2,0,1:T(8,128)S(1)} all-gather(f32[32,2,32]{2,0,1:T(8,128)S(1)} %convolution_bitcast_fusion.7), channel_id=1, replica_groups=mesh['strike'=8,'dev'=64] {'dev'}, dimensions={1}, use_global_device_ids=true | all-gather | bytes 532480 | tf_op jit(solution)/shard_map/all_gather | solution.py:62
  68.5 1.0 convolution_bitcast_fusion.15
  69.5 221.6 %psum.28 = f32[1,32,32]{2,1,0:T(8,128)S(1)} all-reduce(f32[1,32,32]{2,1,0:T(8,128)S(1)} %convolution_bitcast_fusion.15), channel_id=1, replica_groups=mesh['strike'=8,'dev'=64] {'dev'}, use_global_device_ids=true, to_apply=%region_0.3 | all-reduce | flops 1024 | bytes 8192 | tf_op jit(solution)/shard_map/psum | solution.py:63
  291.2 79.8 %all_gather.25 = f32[8,32,32]{2,1,0:T(8,128)S(1)} all-gather(f32[1,32,32]{2,1,0:T(8,128)S(1)} %psum.28), channel_id=1, replica_groups=mesh['strike'=8,'dev'=64] {'strike'}, dimensions={0}, use_global_device_ids=true | all-gather | bytes 36864 | tf_op jit(solution)/shard_map/all_gather | solution.py:64
  371.6 1.4 convolution_bitcast_fusion.3
  374.0 0.8 constant_dynamic-update-slice_fusion.4
  374.8 0.8 constant_dynamic-update-slice_fusion.3
  375.6 0.9 constant_dynamic-update-slice_fusion.2
  376.5 0.8 constant_dynamic-update-slice_fusion.1
  377.2 0.8 constant_dynamic-update-slice_fusion
  378.6 3.0 fusion.8
  381.7 1.2 fusion.53
  382.9 0.8 add_convert_fusion.2
  383.7 1.9 collective-permute-start.4
  385.5 1.9 collective-permute-start.5
  387.4 1.3 collective-permute-start.6
  388.7 1.3 collective-permute-start.7
  390.0 0.9 convolution_bitcast_fusion.6
  390.9 43.2 %all_gather.26 = f32[32,128,32]{2,0,1:T(8,128)S(1)} all-gather(f32[32,2,32]{2,0,1:T(8,128)S(1)} %convolution_bitcast_fusion.6), channel_id=1, replica_groups=mesh['strike'=8,'dev'=64] {'dev'}, dimensions={1}, use_global_device_ids=true | all-gather | bytes 532480 | tf_op jit(solution)/shard_map/all_gather | solution.py:62
  435.0 1.4 convolution_bitcast_fusion.2
  436.4 1.2 fusion.71
  437.6 221.9 %psum.29 = f32[1,32,32]{2,1,0:T(8,128)S(1)} all-reduce(f32[1,32,32]{2,1,0:T(8,128)S(1)} %convolution_bitcast_fusion.14), channel_id=1, replica_groups=mesh['strike'=8,'dev'=64] {'dev'}, use_global_device_ids=true, to_apply=%region_1.4 | all-reduce | flops 1024 | bytes 8192 | tf_op jit(solution)/shard_map/psum | solution.py:63
  659.5 79.5 %all_gather.27 = f32[8,32,32]{2,1,0:T(8,128)S(1)} all-gather(f32[1,32,32]{2,1,0:T(8,128)S(1)} %psum.29), channel_id=1, replica_groups=mesh['strike'=8,'dev'=64] {'strike'}, dimensions={0}, use_global_device_ids=true | all-gather | bytes 36864 | tf_op jit(solution)/shard_map/all_gather | solution.py:64
  739.4 0.8 constant_dynamic-update-slice_fusion.9
  740.2 0.8 constant_dynamic-update-slice_fusion.8
  741.7 0.8 constant_dynamic-update-slice_fusion.6
  742.5 0.8 constant_dynamic-update-slice_fusion.5
  743.9 3.0 fusion.11
  747.0 1.2 fusion.51
  748.2 0.8 add_convert_fusion.1
  749.0 1.9 collective-permute-start.8
  750.9 1.9 collective-permute-start.9
  752.8 1.3 collective-permute-start.10
  754.0 1.3 collective-permute-start.11
  755.3 0.9 convolution_bitcast_fusion.5
  756.2 46.1 %all_gather.28 = f32[32,128,32]{2,0,1:T(8,128)S(1)} all-gather(f32[32,2,32]{2,0,1:T(8,128)S(1)} %convolution_bitcast_fusion.5), channel_id=1, replica_groups=mesh['strike'=8,'dev'=64] {'dev'}, dimensions={1}, use_global_device_ids=true | all-gather | bytes 532480 | tf_op jit(solution)/shard_map/all_gather | solution.py:62
  803.2 1.4 convolution_bitcast_fusion.1
  804.7 1.2 fusion.69
  805.9 221.9 %psum.30 = f32[1,32,32]{2,1,0:T(8,128)S(1)} all-reduce(f32[1,32,32]{2,1,0:T(8,128)S(1)} %convolution_bitcast_fusion.13), channel_id=1, replica_groups=mesh['strike'=8,'dev'=64] {'dev'}, use_global_device_ids=true, to_apply=%region_2.5 | all-reduce | flops 1024 | bytes 8192 | tf_op jit(solution)/shard_map/psum | solution.py:63
  1027.8 79.5 %all_gather.29 = f32[8,32,32]{2,1,0:T(8,128)S(1)} all-gather(f32[1,32,32]{2,1,0:T(8,128)S(1)} %psum.30), channel_id=1, replica_groups=mesh['strike'=8,'dev'=64] {'strike'}, dimensions={0}, use_global_device_ids=true | all-gather | bytes 36864 | tf_op jit(solution)/shard_map/all_gather | solution.py:64
  1107.7 0.8 constant_dynamic-update-slice_fusion.14
  1112.3 3.0 fusion.14
  1115.4 1.2 fusion.49
  1116.6 0.8 multiply_add_fusion
  1117.4 1.9 collective-permute-start.12
  1119.3 1.9 collective-permute-start.13
  1121.2 1.3 collective-permute-start.14
  1122.5 1.3 collective-permute-start.15
  1123.8 0.9 convolution_bitcast_fusion.4
  1124.7 45.8 %all_gather.30 = f32[32,128,32]{2,0,1:T(8,128)S(1)} all-gather(f32[32,2,32]{2,0,1:T(8,128)S(1)} %convolution_bitcast_fusion.4), channel_id=1, replica_groups=mesh['strike'=8,'dev'=64] {'dev'}, dimensions={1}, use_global_device_ids=true | all-gather | bytes 532480 | tf_op jit(solution)/shard_map/all_gather | solution.py:62
  1171.4 1.4 convolution_bitcast_fusion
  1172.8 1.2 fusion.67
  1174.1 221.9 %psum.31 = f32[1,32,32]{2,1,0:T(8,128)S(1)} all-reduce(f32[1,32,32]{2,1,0:T(8,128)S(1)} %convolution_bitcast_fusion.12), channel_id=1, replica_groups=mesh['strike'=8,'dev'=64] {'dev'}, use_global_device_ids=true, to_apply=%region_3.6 | all-reduce | flops 1024 | bytes 8192 | tf_op jit(solution)/shard_map/psum | solution.py:63
  1396.0 79.5 %all_gather.31 = f32[8,32,32]{2,1,0:T(8,128)S(1)} all-gather(f32[1,32,32]{2,1,0:T(8,128)S(1)} %psum.31), channel_id=1, replica_groups=mesh['strike'=8,'dev'=64] {'strike'}, dimensions={0}, use_global_device_ids=true | all-gather | bytes 36864 | tf_op jit(solution)/shard_map/all_gather | solution.py:64
  1475.9 1.6 copy.91
  1482.0 3.0 fusion.17
  1485.1 1.2 fusion.47
  (119 shorter events, 17.9 us)
Async XLA Ops:
  0.6 371.0 %copy-start = (f32[1,32,32,32]{3,2,1,0:T(8,128)S(1)}, f32[1,32,32,32]{3,2,1,0:T(8,128)}, u32[]{:S(2)}) copy-start(f32[1,32,32,32]{3,2,1,0:T(8,128)} %param.28) | copy-start | bytes 393220
  0.6 372.4 %copy-start.16 = (s32[1,32]{1,0:T(1,128)S(1)}, s32[1,32]{1,0:T(1,128)}, u32[]{:S(2)}) copy-start(s32[1,32]{1,0:T(1,128)} %param.27) | copy-start | bytes 388
  0.7 372.9 %copy-start.1 = (f32[2,8,32,32]{3,2,1,0:T(8,128)S(1)}, f32[2,8,32,32]{3,2,1,0:T(8,128)}, u32[]{:S(2)}) copy-start(f32[2,8,32,32]{3,2,1,0:T(8,128)} %param.31) | copy-start | bytes 196612
  2.2 371.8 %collective-permute-start = (bf16[32,2,256]{2,0,1:T(8,128)(2,1)}, bf16[32,2,256]{2,0,1:T(8,128)(2,1)}, u32[]{:S(2)}, u32[]{:S(2)}) collective-permute-start(bf16[32,2,256]{2,0,1:T(8,128)(2,1)} %add_convert_fusion.3), channel_id=1, source_target_pairs={{0,2},{1,3},{2,4},{3,5},{4,6},{5,7},{6,8},{7,9},{8,10},{9,11},{10,... | collective-permute-start | bytes 98312 | tf_op jit(solution)/shard_map/ppermute | solution.py:19
  7.8 367.0 %collective-permute-start.1 = (bf16[32,2,256]{2,0,1:T(8,128)(2,1)}, bf16[32,2,256]{2,0,1:T(8,128)(2,1)}, u32[]{:S(2)}, u32[]{:S(2)}) collective-permute-start(bf16[32,2,256]{2,0,1:T(8,128)(2,1)} %add_convert_fusion.3), channel_id=1, source_target_pairs={{0,1},{1,2},{2,3},{3,4},{4,5},{5,6},{6,7},{7,8},{8,9},{9,10},{10,1... | collective-permute-start | bytes 98312 | tf_op jit(solution)/shard_map/ppermute | solution.py:19
  11.6 364.8 %collective-permute-start.2 = (bf16[32,2,256]{2,0,1:T(8,128)(2,1)}, bf16[32,2,256]{2,0,1:T(8,128)(2,1)}, u32[]{:S(2)}, u32[]{:S(2)}) collective-permute-start(bf16[32,2,256]{2,0,1:T(8,128)(2,1)} %add_convert_fusion.3), channel_id=1, source_target_pairs={{1,0},{2,1},{3,2},{4,3},{5,4},{6,5},{7,6},{8,7},{9,8},{10,9},{11,1... | collective-permute-start | bytes 98312 | tf_op jit(solution)/shard_map/ppermute | solution.py:19
  12.9 364.3 %collective-permute-start.3 = (bf16[32,2,256]{2,0,1:T(8,128)(2,1)}, bf16[32,2,256]{2,0,1:T(8,128)(2,1)}, u32[]{:S(2)}, u32[]{:S(2)}) collective-permute-start(bf16[32,2,256]{2,0,1:T(8,128)(2,1)} %add_convert_fusion.3), channel_id=1, source_target_pairs={{2,0},{3,1},{4,2},{5,3},{6,4},{7,5},{8,6},{9,7},{10,8},{11,9},{12,... | collective-permute-start | bytes 98312 | tf_op jit(solution)/shard_map/ppermute | solution.py:19
  16.8 374.1 %copy-start.5 = (pred[32]{0:T(512)(128)(4,1)}, pred[32]{0:T(512)(128)(4,1)S(1)}, u32[]{:S(2)}) copy-start(pred[32]{0:T(512)(128)(4,1)S(1)} %get-tuple-element.6) | copy-start | bytes 100
  16.8 364.8 %copy-start.6 = (s32[1024]{0:T(1024)}, s32[1024]{0:T(1024)S(1)}, u32[]{:S(2)}) copy-start(s32[1024]{0:T(1024)S(1)} %pad_clamp_fusion.1) | copy-start | bytes 12292
  68.5 313.1 %copy-start.7 = (s32[1024]{0:T(1024)}, s32[1024]{0:T(1024)S(1)}, u32[]{:S(2)}) copy-start(s32[1024]{0:T(1024)S(1)} %pad_clamp_fusion) | copy-start | bytes 12292
  373.0 8.7 copy-start.8
  373.9 8.9 copy-start.2
  374.0 8.9 copy-start.4
  374.0 8.9 copy-start.17
  374.0 8.9 copy-start.21
  374.0 8.9 copy-start.25
  374.0 9.6 copy-start.12
  378.6 55.5 %copy-start.3 = (f32[2,32,32]{2,1,0:T(8,128)S(1)}, f32[2,32,32]{2,1,0:T(8,128)}, u32[]{:S(2)}) copy-start(f32[2,32,32]{2,1,0:T(8,128)} %param.30) | copy-start | bytes 24580
  383.7 355.7 %collective-permute-start.4 = (bf16[32,2,256]{2,0,1:T(8,128)(2,1)}, bf16[32,2,256]{2,0,1:T(8,128)(2,1)}, u32[]{:S(2)}, u32[]{:S(2)}) collective-permute-start(bf16[32,2,256]{2,0,1:T(8,128)(2,1)} %get-tuple-element.10), channel_id=1, source_target_pairs={{0,2},{1,3},{2,4},{3,5},{4,6},{5,7},{6,8},{7,9},{8,10},{9,11},{10,... | collective-permute-start | bytes 98312 | tf_op jit(solution)/shard_map/ppermute | solution.py:19
  385.5 354.6 %collective-permute-start.5 = (bf16[32,2,256]{2,0,1:T(8,128)(2,1)}, bf16[32,2,256]{2,0,1:T(8,128)(2,1)}, u32[]{:S(2)}, u32[]{:S(2)}) collective-permute-start(bf16[32,2,256]{2,0,1:T(8,128)(2,1)} %get-tuple-element.10), channel_id=1, source_target_pairs={{0,1},{1,2},{2,3},{3,4},{4,5},{5,6},{6,7},{7,8},{8,9},{9,10},{10,1... | collective-permute-start | bytes 98312 | tf_op jit(solution)/shard_map/ppermute | solution.py:19
  387.4 354.3 %collective-permute-start.6 = (bf16[32,2,256]{2,0,1:T(8,128)(2,1)}, bf16[32,2,256]{2,0,1:T(8,128)(2,1)}, u32[]{:S(2)}, u32[]{:S(2)}) collective-permute-start(bf16[32,2,256]{2,0,1:T(8,128)(2,1)} %get-tuple-element.10), channel_id=1, source_target_pairs={{1,0},{2,1},{3,2},{4,3},{5,4},{6,5},{7,6},{8,7},{9,8},{10,9},{11,1... | collective-permute-start | bytes 98312 | tf_op jit(solution)/shard_map/ppermute | solution.py:19
  388.7 353.8 %collective-permute-start.7 = (bf16[32,2,256]{2,0,1:T(8,128)(2,1)}, bf16[32,2,256]{2,0,1:T(8,128)(2,1)}, u32[]{:S(2)}, u32[]{:S(2)}) collective-permute-start(bf16[32,2,256]{2,0,1:T(8,128)(2,1)} %get-tuple-element.10), channel_id=1, source_target_pairs={{2,0},{3,1},{4,2},{5,3},{6,4},{7,5},{8,6},{9,7},{10,8},{11,9},{12,... | collective-permute-start | bytes 98312 | tf_op jit(solution)/shard_map/ppermute | solution.py:19
  436.4 310.6 %copy-start.9 = (s32[1,32]{1,0:T(1,128)S(1)}, s32[1,32]{1,0:T(1,128)}, u32[]{:S(2)}) copy-start(s32[1,32]{1,0:T(1,128)} %param.23) | copy-start | bytes 388
  436.4 310.6 %copy-start.13 = (f32[32]{0:T(128)S(1)}, f32[32]{0:T(128)}, u32[]{:S(2)}) copy-start(f32[32]{0:T(128)} %copy-done.12) | copy-start | bytes 388
  739.3 8.9 copy-start.18
  739.3 8.9 copy-start.22
  739.3 8.9 copy-start.26
  739.4 8.9 copy-start.29
  749.0 358.7 %collective-permute-start.8 = (bf16[32,2,256]{2,0,1:T(8,128)(2,1)}, bf16[32,2,256]{2,0,1:T(8,128)(2,1)}, u32[]{:S(2)}, u32[]{:S(2)}) collective-permute-start(bf16[32,2,256]{2,0,1:T(8,128)(2,1)} %get-tuple-element.12), channel_id=1, source_target_pairs={{0,2},{1,3},{2,4},{3,5},{4,6},{5,7},{6,8},{7,9},{8,10},{9,11},{10,... | collective-permute-start | bytes 98312 | tf_op jit(solution)/shard_map/ppermute | solution.py:19
  750.9 357.7 %collective-permute-start.9 = (bf16[32,2,256]{2,0,1:T(8,128)(2,1)}, bf16[32,2,256]{2,0,1:T(8,128)(2,1)}, u32[]{:S(2)}, u32[]{:S(2)}) collective-permute-start(bf16[32,2,256]{2,0,1:T(8,128)(2,1)} %get-tuple-element.12), channel_id=1, source_target_pairs={{0,1},{1,2},{2,3},{3,4},{4,5},{5,6},{6,7},{7,8},{8,9},{9,10},{10,1... | collective-permute-start | bytes 98312 | tf_op jit(solution)/shard_map/ppermute | solution.py:19
  752.8 357.3 %collective-permute-start.10 = (bf16[32,2,256]{2,0,1:T(8,128)(2,1)}, bf16[32,2,256]{2,0,1:T(8,128)(2,1)}, u32[]{:S(2)}, u32[]{:S(2)}) collective-permute-start(bf16[32,2,256]{2,0,1:T(8,128)(2,1)} %get-tuple-element.12), channel_id=1, source_target_pairs={{1,0},{2,1},{3,2},{4,3},{5,4},{6,5},{7,6},{8,7},{9,8},{10,9},{11,1... | collective-permute-start | bytes 98312 | tf_op jit(solution)/shard_map/ppermute | solution.py:19
  754.0 356.8 %collective-permute-start.11 = (bf16[32,2,256]{2,0,1:T(8,128)(2,1)}, bf16[32,2,256]{2,0,1:T(8,128)(2,1)}, u32[]{:S(2)}, u32[]{:S(2)}) collective-permute-start(bf16[32,2,256]{2,0,1:T(8,128)(2,1)} %get-tuple-element.12), channel_id=1, source_target_pairs={{2,0},{3,1},{4,2},{5,3},{6,4},{7,5},{8,6},{9,7},{10,8},{11,9},{12,... | collective-permute-start | bytes 98312 | tf_op jit(solution)/shard_map/ppermute | solution.py:19
  804.6 310.7 %copy-start.10 = (s32[1,32]{1,0:T(1,128)S(1)}, s32[1,32]{1,0:T(1,128)}, u32[]{:S(2)}) copy-start(s32[1,32]{1,0:T(1,128)} %param.23) | copy-start | bytes 388
  804.6 310.7 %copy-start.14 = (f32[32]{0:T(128)S(1)}, f32[32]{0:T(128)}, u32[]{:S(2)}) copy-start(f32[32]{0:T(128)} %copy-done.12) | copy-start | bytes 388
  1107.7 8.9 copy-start.19
  1107.7 8.9 copy-start.23
  1107.7 8.9 copy-start.27
  1107.7 8.9 copy-start.30
  1107.7 8.9 copy-start.32
  1117.4 360.1 %collective-permute-start.12 = (bf16[32,2,256]{2,0,1:T(8,128)(2,1)}, bf16[32,2,256]{2,0,1:T(8,128)(2,1)}, u32[]{:S(2)}, u32[]{:S(2)}) collective-permute-start(bf16[32,2,256]{2,0,1:T(8,128)(2,1)} %get-tuple-element.9), channel_id=1, source_target_pairs={{0,2},{1,3},{2,4},{3,5},{4,6},{5,7},{6,8},{7,9},{8,10},{9,11},{10,... | collective-permute-start | bytes 98312 | tf_op jit(solution)/shard_map/ppermute | solution.py:19
  1119.3 358.9 %collective-permute-start.13 = (bf16[32,2,256]{2,0,1:T(8,128)(2,1)}, bf16[32,2,256]{2,0,1:T(8,128)(2,1)}, u32[]{:S(2)}, u32[]{:S(2)}) collective-permute-start(bf16[32,2,256]{2,0,1:T(8,128)(2,1)} %get-tuple-element.9), channel_id=1, source_target_pairs={{0,1},{1,2},{2,3},{3,4},{4,5},{5,6},{6,7},{7,8},{8,9},{9,10},{10,1... | collective-permute-start | bytes 98312 | tf_op jit(solution)/shard_map/ppermute | solution.py:19
  1121.2 358.6 %collective-permute-start.14 = (bf16[32,2,256]{2,0,1:T(8,128)(2,1)}, bf16[32,2,256]{2,0,1:T(8,128)(2,1)}, u32[]{:S(2)}, u32[]{:S(2)}) collective-permute-start(bf16[32,2,256]{2,0,1:T(8,128)(2,1)} %get-tuple-element.9), channel_id=1, source_target_pairs={{1,0},{2,1},{3,2},{4,3},{5,4},{6,5},{7,6},{8,7},{9,8},{10,9},{11,1... | collective-permute-start | bytes 98312 | tf_op jit(solution)/shard_map/ppermute | solution.py:19
  1122.5 358.1 %collective-permute-start.15 = (bf16[32,2,256]{2,0,1:T(8,128)(2,1)}, bf16[32,2,256]{2,0,1:T(8,128)(2,1)}, u32[]{:S(2)}, u32[]{:S(2)}) collective-permute-start(bf16[32,2,256]{2,0,1:T(8,128)(2,1)} %get-tuple-element.9), channel_id=1, source_target_pairs={{2,0},{3,1},{4,2},{5,3},{6,4},{7,5},{8,6},{9,7},{10,8},{11,9},{12,... | collective-permute-start | bytes 98312 | tf_op jit(solution)/shard_map/ppermute | solution.py:19
  1172.8 312.3 %copy-start.11 = (s32[1,32]{1,0:T(1,128)S(1)}, s32[1,32]{1,0:T(1,128)}, u32[]{:S(2)}) copy-start(s32[1,32]{1,0:T(1,128)} %param.23) | copy-start | bytes 388
  1172.8 312.3 %copy-start.15 = (f32[32]{0:T(128)S(1)}, f32[32]{0:T(128)}, u32[]{:S(2)}) copy-start(f32[32]{0:T(128)} %copy-done.12) | copy-start | bytes 388
  1475.8 10.4 copy-start.20
  1475.8 10.4 copy-start.24
  1475.9 10.4 copy-start.28
  1475.9 10.4 copy-start.31
  1475.9 10.4 copy-start.33
  1475.9 10.4 copy-start.34
where the time goes:
time: 1490 us
  blocking collectives  1390 us (93%)
  matrix products  35.6 us (2%)
  starting transfers between devices  31 us (2%)
  local copies, waits for them, and re-layouts  22.4 us (2%)
    psum x4, blocking collectives, slopes(): group_total = lax.psum(group_part, 'dev')  887 us
    all_gather x4, blocking collectives, slopes(): all_groups = lax.all_gather(group_total[None], 'strike', axis=0, tiled=True)  318 us
    all_gather x4, blocking collectives, slopes(): all_coefs = lax.all_gather(coefs, 'dev', axis=1, tiled=True)  185 us
    ppermute x16, starting transfers between devices, from_behind(): return lax.ppermute(block, axis, route)  31 us
  transfers between devices with their start and end apart: 16, of which 0 were waited for; matrix products, arithmetic and copies ran while one was open for 2% of the time, Pallas kernels for 0%

commit v1 on v0

v1 whole, which is shorter than its diff:
```python
import jax
import jax.numpy as jnp
from jax import lax
from jax.experimental import pallas as pl
from jax.experimental.pallas import tpu as pltpu
from jax.sharding import PartitionSpec as P

CL = 2
NB = 32
NF = 32
REACH = 2
E = 32
R = 32
PS = 256
SIDE = 8
STAGES = 4
Q = 4
ROWS = R // Q

time_step = 0.25
viscous = 0.5
highest = lax.Precision.HIGHEST
f32 = jnp.float32
bf16 = jnp.bfloat16


def split(x):
    hi = lax.reduce_precision(x, 8, 7)
    return hi.astype(bf16), (x - hi).astype(bf16)


def pick_blocks(x, rows):
    block = lax.broadcasted_iota(jnp.int32, (rows, 128), 1) // E
    out = x[0:rows]
    for q in range(1, Q):
        out = jnp.where(block == q, x[q * rows : (q + 1) * rows], out)
    return out


def kernel(
    near_at,
    near_to,
    far_at,
    u_in,
    s_in,
    a_ref,
    b_ref,
    blocks_hbm,
    w1_ref,
    far_ref,
    coarse_ref,
    bases_ref,
    u_out,
    s_out,
    blocks,
    u_now,
    s_now,
    u_sum,
    s_sum,
    tab_a,
    tab_b,
    tab_p,
    tab_c,
    tab_n,
    work_n,
    work_b,
    x_far,
    load_sem,
    a_send,
    a_recv,
    b_send,
    b_recv,
    p_send,
    p_recv,
    c_send,
    c_recv,
    n_send,
    n_recv,
):
    st = lax.axis_index("strike")
    dv = lax.axis_index("dev")
    core = lax.rem(st, 2)
    z = lax.div(dv, SIDE)
    y = lax.rem(dv, SIDE)
    my_a = y + core * (z - y)
    my_b = z + core * (y - z)
    step_a = 1 + (SIDE - 1) * core
    step_b = SIDE - (SIDE - 1) * core

    def on_a(d):
        return (st, lax.rem(my_a + d, SIDE) * step_a + my_b * step_b)

    def on_b(d):
        return (st, my_a * step_a + lax.rem(my_b + d, SIDE) * step_b)

    def on_strike(d):
        return (lax.rem(st + d, SIDE), dv)

    offsets = [o for o in range(-REACH, REACH + 1) if o != 0]

    def has(o):
        return (dv + o >= 0) & (dv + o < SIDE * SIDE)

    load = pltpu.make_async_copy(blocks_hbm, blocks, load_sem)
    load.start()

    tab_n[...] = jnp.zeros_like(tab_n)

    barrier = pltpu.get_barrier_semaphore()
    for d in range(1, SIDE):
        for to in (on_a(d), on_b(d), on_strike(d)):
            pl.semaphore_signal(barrier, inc=1, device_id=to)
    n_near = jnp.int32(0)
    for o in offsets:
        n_near = n_near + has(o).astype(jnp.int32)

        @pl.when(has(o))
        def _():
            pl.semaphore_signal(barrier, inc=1, device_id=(st, dv + o))

    for c in range(CL):
        u_now[c] = u_in[c]
        s_now[c] = s_in[c]
    u_sum[...] = jnp.zeros_like(u_sum)
    s_sum[...] = jnp.zeros_like(s_sum)

    pl.semaphore_wait(barrier, 3 * (SIDE - 1) + n_near)

    def near_copy(s, o):
        slot = tab_n.at[s, pl.ds((REACH - o) * CL, CL)]
        return pltpu.make_async_remote_copy(
            src_ref=tab_n.at[s, pl.ds(REACH * CL, CL)],
            dst_ref=slot,
            send_sem=n_send.at[s, o + REACH],
            recv_sem=n_recv.at[s, REACH - o],
            device_id=(st, dv + o),
        )

    def send_all(ref, send, recv, to):
        for d in range(1, SIDE):
            pltpu.make_async_remote_copy(
                src_ref=ref, dst_ref=ref, send_sem=send, recv_sem=recv, device_id=to(d)
            ).start()

    def wait_bytes(ref, sem):
        part = ref.at[pl.ds(0, SIDE - 1)]
        pltpu.make_async_copy(part, part, sem).wait()

    def stage(s, carry):
        for c in range(CL):
            tab_n[s, REACH * CL + c] = (jnp.exp(u_now[c]) - 1.0).astype(bf16)
        outs = []
        for c in range(CL):
            deficit = tab_n[s, REACH * CL + c]
            wide = jnp.concatenate([deficit] * Q, axis=0)
            outs.append(
                lax.dot_general(
                    w1_ref[c], wide, (((1,), (1,)), ((), ())), preferred_element_type=f32
                )
            )
        coefs = jnp.concatenate([pick_blocks(o[0:R], ROWS) for o in outs], axis=0)
        share = outs[0][R : 2 * R] + outs[0][2 * R :] + outs[1][R : 2 * R] + outs[1][2 * R :]
        share = pick_blocks(share, ROWS)
        share_hi = share.astype(bf16).astype(f32)
        tab_a[s, my_a, 0 : 2 * ROWS] = coefs.astype(bf16)
        tab_a[s, my_a, 2 * ROWS : 4 * ROWS] = jnp.concatenate(
            [share_hi, share - share_hi], axis=0
        ).astype(bf16)
        send_all(tab_a.at[s, my_a], a_send.at[s], a_recv.at[s], on_a)
        for o in offsets:

            @pl.when(has(o))
            def _():
                near_copy(s, o).start()

        wait_bytes(tab_a.at[s], a_recv.at[s])
        total = jnp.zeros((2 * ROWS, 128), f32)
        for i in range(SIDE):
            total = total + tab_a[s, i, 2 * ROWS : 4 * ROWS].astype(f32)
        tab_p[s, my_b] = total[0:ROWS] + total[ROWS:]
        send_all(tab_p.at[s, my_b], p_send.at[s], p_recv.at[s], on_b)
        tab_b[s, my_b] = tab_a[s, :, 0 : 2 * ROWS]
        send_all(tab_b.at[s, my_b], b_send.at[s], b_recv.at[s], on_b)

        wait_bytes(tab_p.at[s], p_recv.at[s])
        group = jnp.sum(tab_p[s], axis=0)
        group_hi = group.astype(bf16).astype(f32)
        tab_c[s, st] = jnp.concatenate([group_hi, group - group_hi], axis=0).astype(bf16)
        send_all(tab_c.at[s, st], c_send.at[s], c_recv.at[s], on_strike)

        @pl.when(s == 0)
        def _():
            load.wait()

        for o in offsets:

            @pl.when(has(-o))
            def _():
                near_copy(s, o).wait_recv()

        work_n[...] = tab_n[s]
        near = jnp.zeros((CL * E, PS), f32)
        for k0 in range(0, NB, 4):
            lhs = []
            for k in range(k0, k0 + 4):
                rows = work_n[near_at[k]]
                lhs.append(
                    jnp.concatenate(
                        [rows * jnp.full((E, PS), near_to[c, k], f32).astype(bf16) for c in range(CL)],
                        axis=0,
                    )
                )
            near = near + jnp.dot(
                jnp.concatenate(lhs, axis=1),
                blocks[k0 : k0 + 4].reshape(4 * PS, PS),
                preferred_element_type=f32,
            )

        wait_bytes(tab_b.at[s], b_recv.at[s])
        work_b[...] = tab_b[s].reshape(SIDE * SIDE, 2 * ROWS, 128)
        for k in range(NF):
            x_far[k] = work_b[far_at[k]]
        out = jnp.dot(far_ref[...], x_far[...].reshape(NF * 2 * ROWS, 128), preferred_element_type=f32)
        wait_bytes(tab_c.at[s], c_recv.at[s])
        out = out + jnp.dot(
            coarse_ref[...], tab_c[s].reshape(SIDE * 2 * ROWS, 128), preferred_element_type=f32
        )
        flipped = pick_blocks(out, CL * R).T
        expansion = flipped[0:E] + flipped[E : 2 * E] + flipped[2 * E : 3 * E] + flipped[3 * E :]
        far = jnp.dot(expansion.astype(bf16), bases_ref[...], preferred_element_type=f32)

        weight = jnp.where((s == 1) | (s == 2), 2.0, 1.0).astype(f32)
        ahead = jnp.where(s == 2, time_step, 0.5 * time_step).astype(f32)
        for c in range(CL):
            velocity = jnp.exp(u_now[c])
            stress_rate = -(near[c * E : (c + 1) * E] + far[:, c * PS : (c + 1) * PS])
            ds = jnp.exp(-s_now[c]) - velocity
            du = (stress_rate - b_ref[c : c + 1] * ds) / (a_ref[c : c + 1] + viscous * velocity)
            u_sum[c] += weight * du
            s_sum[c] += weight * ds
            u_now[c] = u_in[c] + ahead * du
            s_now[c] = s_in[c] + ahead * ds

        wait_bytes(tab_a.at[s], a_send.at[s])
        wait_bytes(tab_p.at[s], p_send.at[s])
        wait_bytes(tab_b.at[s], b_send.at[s])
        wait_bytes(tab_c.at[s], c_send.at[s])
        for o in offsets:

            @pl.when(has(o))
            def _():
                near_copy(s, o).wait_send()

        return carry

    lax.fori_loop(0, STAGES, stage, 0)
    for c in range(CL):
        u_out[c] = u_in[c] + (time_step / 6.0) * u_sum[c]
        s_out[c] = s_in[c] + (time_step / 6.0) * s_sum[c]


def per_device(
    log_rate,
    state_log,
    a_coef,
    b_coef,
    near_src,
    near_dst,
    near_count,
    near_blocks,
    far_src,
    far_dst,
    far_coupling,
    cluster_bases,
    transfer,
    coarse_coupling,
):
    dv = lax.axis_index("dev")
    core = lax.axis_index("strike") % 2
    clusters = jnp.arange(CL, dtype=jnp.int32)

    near_at = (near_src[0] // CL - dv + REACH) * CL + near_src[0] % CL
    near_at = jnp.clip(near_at, 0, (2 * REACH + 1) * CL - 1)
    live = jnp.arange(NB, dtype=jnp.int32) < near_count[0]
    near_to = ((near_dst[0][None] == clusters[:, None]) & live[None]).astype(f32)
    owner = far_src[0] // CL
    far_at = jnp.where(core == 1, owner % SIDE * SIDE + owner // SIDE, owner)

    folded = jnp.einsum(
        "crs,crp->csp", transfer, cluster_bases.astype(f32), precision=highest
    )
    w1 = jnp.concatenate([cluster_bases, *split(folded)], axis=1)
    pick = (far_dst[0][:, None] == clusters)[:, :, None] & (far_src[0] % CL == clusters[:, None]).T[:, None, :]
    far_w = far_coupling[0].reshape(NF, Q, ROWS, R).transpose(1, 3, 0, 2)
    far_w = far_w[:, None, :, :, None, :] * pick.astype(f32).transpose(1, 0, 2)[None, :, None, :, :, None]
    far_w = far_w.reshape(Q * CL * R, NF * CL * ROWS).astype(bf16)
    coarse_w = coarse_coupling.reshape(CL, SIDE, Q, ROWS, R).transpose(2, 0, 4, 1, 3)
    coarse_w = jnp.broadcast_to(coarse_w[:, :, :, :, None], (Q, CL, R, SIDE, 2, ROWS))
    coarse_w = coarse_w.reshape(Q * CL * R, SIDE * 2 * ROWS).astype(bf16)
    bases = jnp.einsum("cd,crp->crdp", jnp.eye(CL, dtype=bf16), cluster_bases).reshape(CL * R, CL * PS)

    vmem = pl.BlockSpec(memory_space=pltpu.VMEM)
    smem = pl.BlockSpec(memory_space=pltpu.SMEM)
    state = (CL, E, PS)
    dma = pltpu.SemaphoreType.DMA
    u_new, s_new = pl.pallas_call(
        kernel,
        out_shape=[jax.ShapeDtypeStruct(state, f32)] * 2,
        in_specs=[smem, smem, smem, vmem, vmem, vmem, vmem, pl.BlockSpec(memory_space=pl.ANY)] + [vmem] * 4,
        out_specs=[vmem, vmem],
        scratch_shapes=[
            pltpu.VMEM((NB, PS, PS), bf16),
            pltpu.VMEM(state, f32),
            pltpu.VMEM(state, f32),
            pltpu.VMEM(state, f32),
            pltpu.VMEM(state, f32),
            pltpu.VMEM((STAGES, SIDE, 4 * ROWS, 128), bf16),
            pltpu.VMEM((STAGES, SIDE, SIDE, 2 * ROWS, 128), bf16),
            pltpu.VMEM((STAGES, SIDE, ROWS, 128), f32),
            pltpu.VMEM((STAGES, SIDE, 2 * ROWS, 128), bf16),
            pltpu.VMEM((STAGES, (2 * REACH + 1) * CL, E, PS), bf16),
            pltpu.VMEM(((2 * REACH + 1) * CL, E, PS), bf16),
            pltpu.VMEM((SIDE * SIDE, 2 * ROWS, 128), bf16),
            pltpu.VMEM((NF, 2 * ROWS, 128), bf16),
            dma,
            dma((STAGES,)),
            dma((STAGES,)),
            dma((STAGES,)),
            dma((STAGES,)),
            dma((STAGES,)),
            dma((STAGES,)),
            dma((STAGES,)),
            dma((STAGES,)),
            dma((STAGES, 2 * REACH + 1)),
            dma((STAGES, 2 * REACH + 1)),
        ],
        compiler_params=pltpu.CompilerParams(
            collective_id=0, has_side_effects=True, vmem_limit_bytes=32 * 1024 * 1024
        ),
    )(
        near_at,
        near_to,
        far_at,
        log_rate.transpose(1, 0, 2),
        state_log.transpose(1, 0, 2),
        a_coef,
        b_coef,
        near_blocks[0],
        w1,
        far_w,
        coarse_w,
        bases,
    )
    return u_new.transpose(1, 0, 2), s_new.transpose(1, 0, 2)


def solution(mesh):
    cluster = ("strike", "dev")
    state = P(None, cluster, None)
    placed = (
        state,
        state,
        P(cluster, None),
        P(cluster, None),
        P(cluster, None),
        P(cluster, None),
        P(cluster),
        P(cluster, None, None, None),
        P(cluster, None),
        P(cluster, None),
        P(cluster, None, None, None),
        P(cluster, None, None),
        P(cluster, None, None),
        P(cluster, None, None, None),
    )
    return jax.shard_map(
        per_device, mesh=mesh, in_specs=placed, out_specs=(state, state), check_vma=False
    )
```

time: 1490 us -> 89.4 us (0.06)
  blocking collectives: 1390 us -> 0 us
  Pallas kernels: 0 us -> 74.8 us
  matrix products: 35.6 us -> 0.98 us
  starting transfers between devices: 31 us -> 0 us
  local copies, waits for them, and re-layouts: 22.4 us -> 7.21 us
    psum x4 -> x0, blocking collectives: 887 us -> none  [slopes(): group_total = lax.psum(group_part, 'dev')]
    all_gather x8 -> x0, blocking collectives: 504 us -> none  [the longest x4 318 us: slopes(): all_groups = lax.all_gather(group_total[None], 'strike', axis=0, tiled=True)]
    pallas_call x0 -> x1, Pallas kernels: none -> 74.8 us  [per_device(): pl.pallas_call(kernel, out_shape=[jax.ShapeDtypeStruct(state, f32)] * 2,...]
    dot_general x32 -> x1, matrix products: 35.6 us -> 0.98 us  [per_device(): jnp.einsum('crs,crp->csp', transfer, cluster_bases.astype(f32), precision...]
    ppermute x16 -> x0, starting transfers between devices: 31 us -> none  [from_behind(): return lax.ppermute(block, axis, route)]
  transfers between devices with their start and end apart: 16 -> 0, of which waited for: 0 -> 0; matrix products, arithmetic and copies ran while one was open for 2% -> 0% of each run, Pallas kernels for 0% -> 0%
where the time goes in v1:
time: 89.4 us; the launch traced here: 88.9 us
  Pallas kernels  74.8 us (84%)
  local copies, waits for them, and re-layouts  7.21 us (8%)
  other arithmetic  4.44 us (5%)
  between operations  1.5 us (2%)
  matrix products  0.98 us (1%)
    pallas_call x1, Pallas kernels, per_device(): pl.pallas_call(kernel, out_shape=[jax.ShapeDtypeStruct(state, f32)] * 2,...  74.8 us
    unnamed x17, local copies, waits for them, and re-layouts  3.63 us

profile of v1, /device:TPU:1, one launch (start us, length us, event | category | flops | bytes accessed | tf_op | source)
XLA Modules:
  0.0 88.9 jit_solution(1979580568236308493)
XLA Ops:
  0.6 0.0 copy-start
  0.7 0.7 broadcast_select_fusion
  1.4 0.0 copy-done
  1.4 1.0 %reduce-precision_convert_fusion = (bf16[2,32,256]{2,1,0:T(8,128)(2,1)S(1)}, bf16[2,32,256]{2,1,0:T(8,128)(2,1)S(1)}) fusion(f32[2,32,32]{2,1,0:T(8,128)S(1)} %copy-done, bf16[2,32,256]{2,1,0:T(8,128)(2,1)} %param.25), kind=kOutput, calls=%fused_computation.4 | convolution fusion | flops 6356992 | bytes 106496 | tf_op jit(solution)/shard_map/crs,crp->csp/dot_general | solution.py:289
  2.4 0.8 pad_maximum_fusion.w1_ref
  3.2 0.9 copy_bitcast_fusion
  4.0 0.0 copy-start.5
  4.0 1.2 %copy.26 = f32[4,32,32,8]{1,0,3,2:T(4,128)S(1)} copy(f32[4,32,32,8]{1,3,0,2:T(8,128)} %bitcast.59) | data formatting | bytes 262144 | tf_op jit(solution)/shard_map/transpose | solution.py:294
  5.3 0.7 fusion.4
  5.9 0.1 iota_compare_fusion
  6.0 0.7 iota_compare_fusion.1
  6.7 0.1 and_convert_fusion
  6.8 0.0 copy-start.4
  6.9 1.2 %multiply_convert_fusion = bf16[4,2,32,32,2,8]{2,1,0,5,4,3:T(2,128)(2,1)S(1)} fusion(f32[2,32,2]{0,2,1:T(2,128)S(1)} %and_convert_fusion, f32[4,32,32,8]{1,0,3,2:T(4,128)S(1)} %copy.26), kind=kLoop, calls=%fused_computation | loop fusion | flops 262144 | bytes 393728 | tf_op jit(solution)/shard_map/convert_element_type | solution.py:296
  8.1 0.0 copy-start.6
  8.1 0.0 copy-start.2
  8.1 0.0 copy-start.3
  8.2 0.7 convert_element_type.38
  8.9 0.1 copy.28.far_ref
  9.0 0.0 copy-done.5
  9.1 0.1 copy.27
  9.2 0.2 broadcast_in_dim.2
  9.4 0.2 convert_element_type.42
  9.6 0.1 copy.29.coarse_ref
  9.7 0.0 copy-done.4
  9.7 0.1 broadcast_multiply_fusion
  10.5 0.0 copy-done.6
  10.6 0.0 copy-done.2
  10.6 0.0 copy-done.3
  10.6 0.0 copy-start.1
  10.6 2.2 %copy-done.1 = bf16[1,32,256,256]{3,2,1,0:T(8,128)(2,1)S(1)} copy-done((bf16[1,32,256,256]{3,2,1,0:T(8,128)(2,1)S(1)}, bf16[1,32,256,256]{3,2,1,0:T(8,128)(2,1)}, u32[]{:S(2)}) %copy-start.1) | copy-done | bytes 4194328
  12.8 74.8 %shard_map.149 = (f32[2,32,256]{2,1,0:T(8,128)S(1)}, f32[2,32,256]{2,1,0:T(8,128)S(1)}) custom-call(s32[32]{0:T(128)S(1)} %get-tuple-element.15.near_at, f32[2,32]{1,0:T(2,128)S(1)} %and_convert_fusion.1.near_to, s32[32]{0:T(128)S(1)} %get-tuple-element.14.far_at, f32[2,32,256]{2,1,0:T(8,128)S(1)} %get-tuple-element.13.u_in, ...), custom_call_target="tpu_custom_call" | custom-call | tf_op jit(solution)/shard_map/pallas_call | solution.py:306
  87.6 0.7 copy.30
  88.2 0.7 copy.31
  (5 shorter events, 0.0 us)
Async XLA Ops:
  0.6 0.8 copy-start
  4.0 5.0 %copy-start.5 = (f32[2,8,32,32]{3,2,1,0:T(8,128)S(1)}, f32[2,8,32,32]{3,2,1,0:T(8,128)}, u32[]{:S(2)}) copy-start(f32[2,8,32,32]{3,2,1,0:T(8,128)} %param.27) | copy-start | bytes 196612
  6.8 2.9 %copy-start.4 = (bf16[2,32,256]{2,1,0:T(8,128)(2,1)S(1)}, bf16[2,32,256]{2,1,0:T(8,128)(2,1)}, u32[]{:S(2)}) copy-start(bf16[2,32,256]{2,1,0:T(8,128)(2,1)} %param.25) | copy-start | bytes 98308
  8.1 2.4 %copy-start.6 = (s32[1,32]{1,0:T(1,128)S(1)}, s32[1,32]{1,0:T(1,128)}, u32[]{:S(2)}) copy-start(s32[1,32]{1,0:T(1,128)} %param.19) | copy-start | bytes 388
  8.1 2.4 %copy-start.2 = (f32[2,256]{1,0:T(2,128)S(1)}, f32[2,256]{1,0:T(2,128)}, u32[]{:S(2)}) copy-start(f32[2,256]{1,0:T(2,128)} %a_ref.1) | copy-start | bytes 6148
  8.1 2.4 %copy-start.3 = (f32[2,256]{1,0:T(2,128)S(1)}, f32[2,256]{1,0:T(2,128)}, u32[]{:S(2)}) copy-start(f32[2,256]{1,0:T(2,128)} %b_ref.1) | copy-start | bytes 6148
  10.6 2.2 %copy-start.1 = (bf16[1,32,256,256]{3,2,1,0:T(8,128)(2,1)S(1)}, bf16[1,32,256,256]{3,2,1,0:T(8,128)(2,1)}, u32[]{:S(2)}) copy-start(bf16[1,32,256,256]{3,2,1,0:T(8,128)(2,1)} %param.21) | copy-start | bytes 12582916

commit v2 on v1

v2 whole, which is shorter than its diff:
```python
import jax
import jax.numpy as jnp
from jax import lax
from jax.experimental import pallas as pl
from jax.experimental.pallas import tpu as pltpu
from jax.sharding import PartitionSpec as P

CL = 2
NB = 32
NF = 32
REACH = 2
E = 32
R = 32
PS = 256
SIDE = 8
XS = 4
GROUPS = 8
STAGES = 4
HALF = E // 2
PIECE = 4

time_step = 0.25
viscous = 0.5
highest = lax.Precision.HIGHEST
f32 = jnp.float32
bf16 = jnp.bfloat16
i32 = jnp.int32

FAR_FIRST = (4, 3, 5, 2, 6, 1, 7)
OFFSETS = (-2, 2, -1, 1)


def ring(d, size):
    return min(d, size - d)


def split(x):
    hi = x.astype(bf16)
    return hi, (x - hi.astype(f32)).astype(bf16)


def lane_block(rows):
    return lax.broadcasted_iota(i32, (rows, 128), 1) // R


def kernel(
    near_src,
    near_dst,
    near_count,
    far_src,
    far_dst,
    u_hbm,
    s_hbm,
    a_hbm,
    b_hbm,
    blocks_hbm,
    coupling_hbm,
    bases_hbm,
    transfer_hbm,
    coarse_hbm,
    out,
    u_in,
    s_in,
    a_ref,
    b_ref,
    blocks,
    coupling,
    bases,
    transfer,
    coarse,
    near_at,
    near_to,
    far_at,
    w_coefs,
    w_far,
    w_coarse,
    w_bases,
    u_now,
    s_now,
    inverse,
    known,
    tab_a,
    tab_o,
    tab_r,
    tab_b,
    tab_n,
    work_n,
    work_b,
    load_sem,
    a_send,
    a_recv,
    o_send,
    o_recv,
    r_send,
    r_recv,
    b_send,
    b_recv,
    n_send,
    n_recv,
):
    st = lax.axis_index("strike")
    dv = lax.axis_index("dev")
    core = lax.rem(st, 2)
    x = lax.div(st, 2)
    z = lax.div(dv, SIDE)
    y = lax.rem(dv, SIDE)
    other = st + 1 - 2 * core
    my_a = y + core * (z - y)
    my_b = z + core * (y - z)
    step_a = 1 + (SIDE - 1) * core
    step_b = SIDE - (SIDE - 1) * core

    def on_a(d):
        return (st, lax.rem(my_a + d, SIDE) * step_a + my_b * step_b)

    def on_b(d):
        return (st, my_a * step_a + lax.rem(my_b + d, SIDE) * step_b)

    def on_other(d):
        return (other, my_a * step_a + lax.rem(my_b + d, SIDE) * step_b)

    def from_other(d):
        return (other, lax.rem(my_a + d, SIDE) * step_a + my_b * step_b)

    def on_xb(dx, d):
        return (lax.rem(x + dx, XS) * 2 + core, my_a * step_a + lax.rem(my_b + d, SIDE) * step_b)

    far_xb = sorted(
        ((dx, d) for dx in range(XS) for d in range(SIDE) if dx or d),
        key=lambda p: -(ring(p[0], XS) + ring(p[1], SIDE)),
    )

    def has(o):
        return (dv + o >= 0) & (dv + o < SIDE * SIDE)

    loads = [
        (u_hbm.at[:, 0], u_in.at[0]),
        (u_hbm.at[:, 1], u_in.at[1]),
        (bases_hbm, bases),
        (transfer_hbm, transfer),
        (s_hbm.at[:, 0], s_in.at[0]),
        (s_hbm.at[:, 1], s_in.at[1]),
        (a_hbm, a_ref),
        (b_hbm, b_ref),
        (coupling_hbm.at[0], coupling),
        (coarse_hbm, coarse),
        (blocks_hbm.at[0], blocks),
    ]
    loads = [pltpu.make_async_copy(src, dst, load_sem.at[i]) for i, (src, dst) in enumerate(loads)]
    for load in loads:
        load.start()

    tab_n[...] = jnp.zeros_like(tab_n)

    barrier = pltpu.get_barrier_semaphore()
    for dx, d in far_xb:
        pl.semaphore_signal(barrier, inc=1, device_id=on_xb(dx, d))
    for d in FAR_FIRST:
        pl.semaphore_signal(barrier, inc=1, device_id=on_a(d))
    for d in FAR_FIRST + (0,):
        pl.semaphore_signal(barrier, inc=1, device_id=from_other(d))
    n_near = jnp.int32(0)
    for o in OFFSETS:
        n_near = n_near + has(o).astype(i32)

        @pl.when(has(o))
        def _():
            pl.semaphore_signal(barrier, inc=1, device_id=(st, dv + o))

    count = near_count[0]
    for k in range(NB):
        src = near_src[0, k]
        at = (lax.div(src, CL) - dv + REACH) * CL + lax.rem(src, CL)
        near_at[k] = jnp.minimum(jnp.maximum(at, 0), (2 * REACH + 1) * CL - 1)
        for c in range(CL):
            near_to[c, k] = jnp.where((near_dst[0, k] == c) & (count > k), 1.0, 0.0).astype(f32)
    for k in range(NF):
        owner = lax.div(far_src[0, k], CL)
        turned = lax.rem(owner, SIDE) * SIDE + lax.div(owner, SIDE)
        far_at[k] = owner + core * (turned - owner)

    for load in loads[:4]:
        load.wait()

    for c in range(CL):
        row = lax.broadcasted_iota(i32, (R, 128), 0)
        lane = lax.broadcasted_iota(i32, (R, 128), 1)
        placed = ((lane % R == row) & ((lane // R) % CL == c)).astype(f32)
        right = jnp.concatenate([placed] + [transfer[c]] * 4, axis=1)
        w_coefs[c * PS : (c + 1) * PS] = lax.dot_general(
            bases[c].astype(f32), right, (((0,), (0,)), ((), ())), precision=highest, preferred_element_type=f32
        ).astype(bf16)

    for c in range(CL):
        u_now[c] = u_in[c]
    out[...] = jnp.zeros_like(out)

    def prepare():
        for load in loads[4:]:
            load.wait()
        for c in range(CL):
            s_now[c] = s_in[c]
            hi, lo = split(
                jnp.dot(
                    coarse[c].reshape(GROUPS * R, R), bases[c].astype(f32), precision=highest, preferred_element_type=f32
                )
            )
            w_coarse[0 : GROUPS * R, c * PS : (c + 1) * PS] = hi
            w_coarse[GROUPS * R :, c * PS : (c + 1) * PS] = lo
        w_bases[...] = jnp.zeros_like(w_bases)
        for half in range(2):
            for c in range(CL):
                j = half * CL + c
                w_bases[j * R : (j + 1) * R, j * PS : (j + 1) * PS] = bases[c]
        block = lane_block(R)
        for k in range(NF):
            wide = jnp.concatenate([coupling[k]] * 4, axis=1)
            for half in range(2):
                for c in range(CL):
                    lanes = jnp.where(lax.rem(far_src[0, k], CL) == c, half * CL + far_dst[0, k], -1)
                    hi, lo = split(jnp.where(block == lanes, wide, 0.0))
                    at = k * 128 + (half * CL + c) * R
                    w_far[0, at : at + R] = hi
                    w_far[1, at : at + R] = lo

    def near_copy(s, o):
        return pltpu.make_async_remote_copy(
            src_ref=tab_n.at[s, pl.ds(REACH * CL, CL)],
            dst_ref=tab_n.at[s, pl.ds((REACH - o) * CL, CL)],
            send_sem=n_send.at[s, o + REACH],
            recv_sem=n_recv.at[s, REACH - o],
            device_id=(st, dv + o),
        )

    def push(src, dst, send, recv, to):
        pltpu.make_async_remote_copy(
            src_ref=src, dst_ref=dst, send_sem=send, recv_sem=recv, device_id=to
        ).start()

    def wait_blocks(ref, n, sem):
        part = ref.at[pl.ds(0, n)]
        pltpu.make_async_copy(part, part, sem).wait()

    def stage(s, carry):
        for c in range(CL):
            tab_n[s, REACH * CL + c] = (jnp.exp(u_now[c]) - 1.0).astype(bf16)
        deficit = jnp.concatenate([tab_n[s, REACH * CL + c] for c in range(CL)], axis=1)
        both = jnp.dot(deficit, w_coefs[...], preferred_element_type=f32)
        block = lane_block(HALF)
        coefs = jnp.where(block < CL, both[0:HALF, 0:128], both[HALF:E, 0:128])
        share = jnp.where(block == core, both[0:HALF, 128:256], 0.0)
        share = jnp.where(block == CL + core, both[HALF:E, 128:256], share)
        tab_a[s, my_a, 0:HALF] = coefs.astype(bf16)
        tab_a[s, my_a, HALF:E] = share.astype(bf16)
        mine = tab_a.at[s, my_a]
        for d in FAR_FIRST:
            push(mine, mine, a_send.at[s], a_recv.at[s], on_a(d))
            push(mine.at[pl.ds(HALF, HALF)], tab_o.at[s, my_b], o_send.at[s], o_recv.at[s], on_other(d))
        push(mine.at[pl.ds(HALF, HALF)], tab_o.at[s, my_b], o_send.at[s], o_recv.at[s], on_other(0))
        for o in OFFSETS:

            @pl.when(has(o))
            def _():
                near_copy(s, o).start()

        pl.when(s == 0)(prepare)

        wait_blocks(tab_a.at[s], SIDE - 1, a_recv.at[s])
        wait_blocks(tab_o.at[s], SIDE, o_recv.at[s])
        total = jnp.zeros((HALF, 128), f32)
        for i in range(SIDE):
            total = total + tab_a[s, i, HALF:E].astype(f32) + tab_o[s, i].astype(f32)
        tab_r[s, x, my_b] = total.astype(bf16)
        mine = tab_r.at[s, x, my_b]
        for dx, d in far_xb:
            push(mine, mine, r_send.at[s], r_recv.at[s], on_xb(dx, d))
        tab_b[s, my_b] = tab_a[s, :, 0:HALF]
        mine = tab_b.at[s, my_b]
        for d in FAR_FIRST:
            push(mine, mine, b_send.at[s], b_recv.at[s], on_b(d))

        for o in OFFSETS:

            @pl.when(has(-o))
            def _():
                near_copy(s, o).wait_recv()

        work_n[...] = tab_n[s]
        near = jnp.zeros((CL * E, PS), f32)
        for k0 in range(0, NB, PIECE):
            lhs = []
            for k in range(k0, k0 + PIECE):
                rows = work_n[near_at[k]]
                lhs.append(
                    jnp.concatenate(
                        [rows * jnp.full((E, PS), near_to[c, k], f32).astype(bf16) for c in range(CL)],
                        axis=0,
                    )
                )
            near = near + jnp.dot(
                jnp.concatenate(lhs, axis=1),
                blocks[k0 : k0 + PIECE].reshape(PIECE * PS, PS),
                preferred_element_type=f32,
            )

        ahead = jnp.where(s == 2, time_step, 0.5 * time_step).astype(f32)
        weight = jnp.where((s == 1) | (s == 2), 2.0, 1.0).astype(f32)
        for c in range(CL):
            velocity = jnp.exp(u_now[c])
            ds = jnp.exp(-s_now[c]) - velocity
            out[1, c] += weight * ds
            s_now[c] = s_in[c] + ahead * ds
            inverse[c] = 1.0 / (a_ref[c : c + 1] + viscous * velocity)
            known[c] = near[c * E : (c + 1) * E] + b_ref[c : c + 1] * ds

        wait_blocks(tab_b.at[s], SIDE - 1, b_recv.at[s])
        work_b[...] = tab_b[s].reshape(SIDE * SIDE, HALF, 128)
        sources = jnp.concatenate([work_b[far_at[k]] for k in range(NF)], axis=1)
        expansion = jnp.dot(sources, w_far[0], preferred_element_type=f32) + jnp.dot(
            sources, w_far[1], preferred_element_type=f32
        )
        far = jnp.dot(expansion.astype(bf16), w_bases[...], preferred_element_type=f32)
        for c in range(CL):
            for half in range(2):
                j = half * CL + c
                known[c, half * HALF : (half + 1) * HALF] += far[:, j * PS : (j + 1) * PS]

        wait_blocks(tab_r.at[s].reshape(XS * SIDE, HALF, 128), XS * SIDE - 1, r_recv.at[s])
        low = block < CL
        sums = [jnp.sum(tab_r[s, i].astype(f32), axis=0) for i in range(XS)]
        turned = [pltpu.roll(v, 64, 1) for v in sums]
        rows = []
        for half in range(2):
            first, second = (sums, turned) if half == 0 else (turned, sums)
            rows.append(
                jnp.concatenate(
                    [jnp.where(low, first[2 * t], second[2 * t + 1]) for t in range(XS // 2)], axis=1
                )
            )
        groups = jnp.concatenate(rows, axis=0).astype(bf16)
        coarse_far = jnp.dot(
            jnp.concatenate([groups, groups], axis=1), w_coarse[...], preferred_element_type=f32
        )
        for c in range(CL):
            du = -(known[c] + coarse_far[:, c * PS : (c + 1) * PS]) * inverse[c]
            u_now[c] = u_in[c] + ahead * du
            out[0, c] += weight * du

        wait_blocks(tab_a.at[s], SIDE - 1, a_send.at[s])
        wait_blocks(tab_o.at[s], SIDE, o_send.at[s])
        wait_blocks(tab_r.at[s].reshape(XS * SIDE, HALF, 128), XS * SIDE - 1, r_send.at[s])
        wait_blocks(tab_b.at[s], SIDE - 1, b_send.at[s])
        for o in OFFSETS:

            @pl.when(has(o))
            def _():
                near_copy(s, o).wait_send()

        return carry

    pl.semaphore_wait(barrier, XS * SIDE - 1 + 2 * SIDE - 1 + n_near)
    lax.fori_loop(0, STAGES, stage, 0)


def per_device(
    log_rate,
    state_log,
    a_coef,
    b_coef,
    near_src,
    near_dst,
    near_count,
    near_blocks,
    far_src,
    far_dst,
    far_coupling,
    cluster_bases,
    transfer,
    coarse_coupling,
):
    vmem = pl.BlockSpec(memory_space=pltpu.VMEM)
    smem = pl.BlockSpec(memory_space=pltpu.SMEM)
    hbm = pl.BlockSpec(memory_space=pl.ANY)
    state = (CL, E, PS)
    dma = pltpu.SemaphoreType.DMA
    sums = pl.pallas_call(
        kernel,
        out_shape=jax.ShapeDtypeStruct((2, *state), f32),
        in_specs=[smem] * 5 + [hbm] * 9,
        out_specs=vmem,
        scratch_shapes=[
            pltpu.VMEM(state, f32),
            pltpu.VMEM(state, f32),
            pltpu.VMEM((CL, PS), f32),
            pltpu.VMEM((CL, PS), f32),
            pltpu.VMEM((NB, PS, PS), bf16),
            pltpu.VMEM((NF, R, R), f32),
            pltpu.VMEM((CL, R, PS), bf16),
            pltpu.VMEM((CL, R, R), f32),
            pltpu.VMEM((CL, GROUPS, R, R), f32),
            pltpu.SMEM((NB,), i32),
            pltpu.SMEM((CL, NB), f32),
            pltpu.SMEM((NF,), i32),
            pltpu.VMEM((CL * PS, 256), bf16),
            pltpu.VMEM((2, NF * 128, 128), bf16),
            pltpu.VMEM((2 * GROUPS * R, CL * PS), bf16),
            pltpu.VMEM((2 * CL * R, 2 * CL * PS), bf16),
            pltpu.VMEM(state, f32),
            pltpu.VMEM(state, f32),
            pltpu.VMEM(state, f32),
            pltpu.VMEM(state, f32),
            pltpu.VMEM((STAGES, SIDE, E, 128), bf16),
            pltpu.VMEM((STAGES, SIDE, HALF, 128), bf16),
            pltpu.VMEM((STAGES, XS, SIDE, HALF, 128), bf16),
            pltpu.VMEM((STAGES, SIDE, SIDE, HALF, 128), bf16),
            pltpu.VMEM((STAGES, (2 * REACH + 1) * CL, E, PS), bf16),
            pltpu.VMEM(((2 * REACH + 1) * CL, E, PS), bf16),
            pltpu.VMEM((SIDE * SIDE, HALF, 128), bf16),
            dma((11,)),
        ]
        + [dma((STAGES,))] * 8
        + [dma((STAGES, 2 * REACH + 1))] * 2,
        compiler_params=pltpu.CompilerParams(
            collective_id=0, has_side_effects=True, vmem_limit_bytes=56 * 1024 * 1024
        ),
    )(
        near_src,
        near_dst,
        near_count,
        far_src,
        far_dst,
        log_rate,
        state_log,
        a_coef,
        b_coef,
        near_blocks,
        far_coupling,
        cluster_bases,
        transfer,
        coarse_coupling,
    )
    sums = (time_step / 6.0) * sums.transpose(0, 2, 1, 3)
    return log_rate + sums[0], state_log + sums[1]


def solution(mesh):
    cluster = ("strike", "dev")
    state = P(None, cluster, None)
    placed = (
        state,
        state,
        P(cluster, None),
        P(cluster, None),
        P(cluster, None),
        P(cluster, None),
        P(cluster),
        P(cluster, None, None, None),
        P(cluster, None),
        P(cluster, None),
        P(cluster, None, None, None),
        P(cluster, None, None),
        P(cluster, None, None),
        P(cluster, None, None, None),
    )
    return jax.shard_map(
        per_device, mesh=mesh, in_specs=placed, out_specs=(state, state), check_vma=False
    )
```

time: 89.4 us -> 75.1 us (0.84)
  local copies, waits for them, and re-layouts: 7.21 us -> 1.37 us
  Pallas kernels: 74.8 us -> 71.2 us
  other arithmetic: 4.44 us -> 0.94 us
  matrix products: 0.98 us -> 0 us
    pallas_call x1, Pallas kernels: 74.8 us -> 71.2 us  [per_device(): pl.pallas_call(kernel, out_shape=jax.ShapeDtypeStruct((2, *state), f32),...]
    unnamed x17 -> x6, local copies, waits for them, and re-layouts: 3.63 us -> 1.37 us
    transpose x2 -> x0, local copies, waits for them, and re-layouts: 2.1 us -> none  [the longest x1 1.22 us: per_device(): far_w = far_coupling[0].reshape(NF, Q, ROWS, R).transpose(1, 3, 0, 2)]
    eq x3 -> x0, other arithmetic: 1.47 us -> none  [the longest x2 0.74 us: per_device(): far_src[0] % CL == clusters[:, None]]
    convert_element_type x4 -> x0, other arithmetic: 1.38 us -> none  [the longest x1 1.25 us: per_device(): far_w = far_w.reshape(Q * CL * R, NF * CL * ROWS).astype(bf16)]
    convert_element_type x5 -> x0, local copies, waits for them, and re-layouts: 1.28 us -> none  [the longest x2 0.85 us: per_device(): far_w = far_w.reshape(Q * CL * R, NF * CL * ROWS).astype(bf16)]
    dot_general x1 -> x0, matrix products: 0.98 us -> none  [per_device(): jnp.einsum('crs,crp->csp', transfer, cluster_bases.astype(f32), precision...]
    mul x0 -> x1, other arithmetic: none -> 0.92 us  [per_device(): sums = time_step / 6.0 * sums.transpose(0, 2, 1, 3)]
where the time goes in v2:
time: 75.1 us; the launch traced here: 74.9 us
  Pallas kernels  71.2 us (95%)
  local copies, waits for them, and re-layouts  1.37 us (2%)
  between operations  1.37 us (2%)
  other arithmetic  0.94 us (1%)
    pallas_call x1, Pallas kernels, per_device(): pl.pallas_call(kernel, out_shape=jax.ShapeDtypeStruct((2, *state), f32),...  71.2 us

profile of v2, /device:TPU:1, one launch (start us, length us, event | category | flops | bytes accessed | tf_op | source)
XLA Modules:
  0.0 74.9 jit_solution(15364830385133173046)
XLA Ops:
  0.6 0.0 copy-start.1
  0.6 0.0 copy-start
  1.3 71.2 %shard_map.149 = f32[2,2,32,256]{3,2,1,0:T(8,128)} custom-call(s32[1,32]{1,0:T(1,128)} %near_src.1, s32[1,32]{1,0:T(1,128)} %near_dst.1, s32[1]{0:T(128)S(6)} %copy.22.near_count, s32[1,32]{1,0:T(1,128)} %far_src.1, s32[1,32]{1,0:T(1,128)} %far_dst.1, f32[32,2,256]{2,1,0:T(2,128)} %u_hbm.1, f32[32,2,256]{2,1,0:T(2,128)} %s_hbm.1, f32[2,256]{1,0:T(2,128)} %a_hbm.1, ...), custom_call_target="tpu_custom_call" | custom-call | tf_op jit(solution)/shard_map/pallas_call | solution.py:386
  72.6 0.9 %multiply_bitcast_fusion = f32[2,32,2,256]{3,1,2,0:T(8,128)S(1)} fusion(f32[2,2,32,256]{3,2,1,0:T(8,128)} %shard_map.149), kind=kLoop, calls=%fused_computation | loop fusion | flops 32768 | bytes 262144 | tf_op jit(solution)/shard_map/mul | solution.py:442
  73.5 0.0 copy-done.1
  73.5 0.0 copy-done
  73.5 0.7 copy.19
  74.2 0.7 copy.18
  (1 shorter events, 0.0 us)
Async XLA Ops:
  0.6 72.8 %copy-start.1 = (f32[32,2,256]{2,1,0:T(2,128)S(1)}, f32[32,2,256]{2,1,0:T(2,128)}, u32[]{:S(2)}) copy-start(f32[32,2,256]{2,1,0:T(2,128)} %s_hbm.1) | copy-start | bytes 196612
  0.6 72.8 %copy-start = (f32[32,2,256]{2,1,0:T(2,128)S(1)}, f32[32,2,256]{2,1,0:T(2,128)}, u32[]{:S(2)}) copy-start(f32[32,2,256]{2,1,0:T(2,128)} %u_hbm.1) | copy-start | bytes 196612

commit v3 on v2

--- a/solution.py
+++ b/solution.py
@@ -27,11 +27,8 @@
 i32 = jnp.int32
 
 FAR_FIRST = (4, 3, 5, 2, 6, 1, 7)
+X_FIRST = (2, 1, 3)
 OFFSETS = (-2, 2, -1, 1)
-
-
-def ring(d, size):
-    return min(d, size - d)
 
 
 def split(x):
@@ -44,11 +41,11 @@
 
 
 def kernel(
-    near_src,
-    near_dst,
-    near_count,
-    far_src,
-    far_dst,
+    near_src_hbm,
+    near_dst_hbm,
+    near_count_hbm,
+    far_src_hbm,
+    far_dst_hbm,
     u_hbm,
     s_hbm,
     a_hbm,
@@ -59,6 +56,11 @@
     transfer_hbm,
     coarse_hbm,
     out,
+    near_src,
+    near_dst,
+    near_count,
+    far_src,
+    far_dst,
     u_in,
     s_in,
     a_ref,
@@ -79,9 +81,12 @@
     s_now,
     inverse,
     known,
+    u_sum,
+    s_sum,
     tab_a,
     tab_o,
-    tab_r,
+    tab_p,
+    tab_x,
     tab_b,
     tab_n,
     work_n,
@@ -91,8 +96,10 @@
     a_recv,
     o_send,
     o_recv,
-    r_send,
-    r_recv,
+    p_send,
+    p_recv,
+    x_send,
+    x_recv,
     b_send,
     b_recv,
     n_send,
@@ -122,22 +129,35 @@
     def from_other(d):
         return (other, lax.rem(my_a + d, SIDE) * step_a + my_b * step_b)
 
-    def on_xb(dx, d):
-        return (lax.rem(x + dx, XS) * 2 + core, my_a * step_a + lax.rem(my_b + d, SIDE) * step_b)
-
-    far_xb = sorted(
-        ((dx, d) for dx in range(XS) for d in range(SIDE) if dx or d),
-        key=lambda p: -(ring(p[0], XS) + ring(p[1], SIDE)),
-    )
+    def on_x(d):
+        return (lax.rem(x + d, XS) * 2 + core, dv)
 
     def has(o):
         return (dv + o >= 0) & (dv + o < SIDE * SIDE)
+
+    partners = [to(d) for d in FAR_FIRST for to in (on_a, from_other, on_b)] + [from_other(0)]
+    partners += [on_x(d) for d in X_FIRST]
+    barrier = pltpu.get_barrier_semaphore()
+    for to in partners:
+        pl.semaphore_signal(barrier, inc=1, device_id=to)
+    n_near = jnp.int32(0)
+    for o in OFFSETS:
+        n_near = n_near + has(o).astype(i32)
+
+        @pl.when(has(o))
+        def _():
+            pl.semaphore_signal(barrier, inc=1, device_id=(st, dv + o))
 
     loads = [
         (u_hbm.at[:, 0], u_in.at[0]),
         (u_hbm.at[:, 1], u_in.at[1]),
         (bases_hbm, bases),
         (transfer_hbm, transfer),
+        (near_src_hbm, near_src),
+        (near_dst_hbm, near_dst),
+        (near_count_hbm, near_count),
+        (far_src_hbm, far_src),
+        (far_dst_hbm, far_dst),
         (s_hbm.at[:, 0], s_in.at[0]),
         (s_hbm.at[:, 1], s_in.at[1]),
         (a_hbm, a_ref),
@@ -150,34 +170,12 @@
     for load in loads:
         load.start()
 
-    tab_n[...] = jnp.zeros_like(tab_n)
-
-    barrier = pltpu.get_barrier_semaphore()
-    for dx, d in far_xb:
-        pl.semaphore_signal(barrier, inc=1, device_id=on_xb(dx, d))
-    for d in FAR_FIRST:
-        pl.semaphore_signal(barrier, inc=1, device_id=on_a(d))
-    for d in FAR_FIRST + (0,):
-        pl.semaphore_signal(barrier, inc=1, device_id=from_other(d))
-    n_near = jnp.int32(0)
     for o in OFFSETS:
-        n_near = n_near + has(o).astype(i32)
-
-        @pl.when(has(o))
+
+        @pl.when(jnp.logical_not(has(o)))
         def _():
-            pl.semaphore_signal(barrier, inc=1, device_id=(st, dv + o))
-
-    count = near_count[0]
-    for k in range(NB):
-        src = near_src[0, k]
-        at = (lax.div(src, CL) - dv + REACH) * CL + lax.rem(src, CL)
-        near_at[k] = jnp.minimum(jnp.maximum(at, 0), (2 * REACH + 1) * CL - 1)
-        for c in range(CL):
-            near_to[c, k] = jnp.where((near_dst[0, k] == c) & (count > k), 1.0, 0.0).astype(f32)
-    for k in range(NF):
-        owner = lax.div(far_src[0, k], CL)
-        turned = lax.rem(owner, SIDE) * SIDE + lax.div(owner, SIDE)
-        far_at[k] = owner + core * (turned - owner)
+            empty = jnp.zeros((STAGES, CL, E, PS), bf16)
+            tab_n[:, (o + REACH) * CL : (o + REACH + 1) * CL] = empty
 
     for load in loads[:4]:
         load.wait()
@@ -193,11 +191,23 @@
 
     for c in range(CL):
         u_now[c] = u_in[c]
-    out[...] = jnp.zeros_like(out)
+    u_sum[...] = jnp.zeros_like(u_sum)
+    s_sum[...] = jnp.zeros_like(s_sum)
 
     def prepare():
         for load in loads[4:]:
             load.wait()
+        count = near_count[0]
+        for k in range(NB):
+            src = near_src[0, k]
+            at = (lax.div(src, CL) - dv + REACH) * CL + lax.rem(src, CL)
+            near_at[k] = jnp.minimum(jnp.maximum(at, 0), (2 * REACH + 1) * CL - 1)
+            for c in range(CL):
+                near_to[c, k] = jnp.where((near_dst[0, k] == c) & (count > k), 1.0, 0.0).astype(f32)
+        for k in range(NF):
+            owner = lax.div(far_src[0, k], CL)
+            turned = lax.rem(owner, SIDE) * SIDE + lax.div(owner, SIDE)
+            far_at[k] = owner + core * (turned - owner)
         for c in range(CL):
             s_now[c] = s_in[c]
             hi, lo = split(
@@ -212,13 +222,13 @@
             for c in range(CL):
                 j = half * CL + c
                 w_bases[j * R : (j + 1) * R, j * PS : (j + 1) * PS] = bases[c]
-        block = lane_block(R)
+        wide_block = lane_block(R)
         for k in range(NF):
             wide = jnp.concatenate([coupling[k]] * 4, axis=1)
             for half in range(2):
                 for c in range(CL):
                     lanes = jnp.where(lax.rem(far_src[0, k], CL) == c, half * CL + far_dst[0, k], -1)
-                    hi, lo = split(jnp.where(block == lanes, wide, 0.0))
+                    hi, lo = split(jnp.where(wide_block == lanes, wide, 0.0))
                     at = k * 128 + (half * CL + c) * R
                     w_far[0, at : at + R] = hi
                     w_far[1, at : at + R] = lo
@@ -241,22 +251,38 @@
         part = ref.at[pl.ds(0, n)]
         pltpu.make_async_copy(part, part, sem).wait()
 
-    def stage(s, carry):
+    block = lane_block(HALF)
+
+    def begin(s):
         for c in range(CL):
             tab_n[s, REACH * CL + c] = (jnp.exp(u_now[c]) - 1.0).astype(bf16)
         deficit = jnp.concatenate([tab_n[s, REACH * CL + c] for c in range(CL)], axis=1)
         both = jnp.dot(deficit, w_coefs[...], preferred_element_type=f32)
-        block = lane_block(HALF)
         coefs = jnp.where(block < CL, both[0:HALF, 0:128], both[HALF:E, 0:128])
         share = jnp.where(block == core, both[0:HALF, 128:256], 0.0)
         share = jnp.where(block == CL + core, both[HALF:E, 128:256], share)
         tab_a[s, my_a, 0:HALF] = coefs.astype(bf16)
         tab_a[s, my_a, HALF:E] = share.astype(bf16)
+
+    def wait_sends(s):
+        wait_blocks(tab_a.at[s], SIDE - 1, a_send.at[s])
+        wait_blocks(tab_o.at[s], SIDE, o_send.at[s])
+        wait_blocks(tab_p.at[s], SIDE - 1, p_send.at[s])
+        wait_blocks(tab_x.at[s], XS - 1, x_send.at[s])
+        wait_blocks(tab_b.at[s], SIDE - 1, b_send.at[s])
+        for o in OFFSETS:
+
+            @pl.when(has(o))
+            def _():
+                near_copy(s, o).wait_send()
+
+    def stage(s, carry):
         mine = tab_a.at[s, my_a]
+        share = mine.at[pl.ds(HALF, HALF)]
         for d in FAR_FIRST:
             push(mine, mine, a_send.at[s], a_recv.at[s], on_a(d))
-            push(mine.at[pl.ds(HALF, HALF)], tab_o.at[s, my_b], o_send.at[s], o_recv.at[s], on_other(d))
-        push(mine.at[pl.ds(HALF, HALF)], tab_o.at[s, my_b], o_send.at[s], o_recv.at[s], on_other(0))
+            push(share, tab_o.at[s, my_b], o_send.at[s], o_recv.at[s], on_other(d))
+        push(share, tab_o.at[s, my_b], o_send.at[s], o_recv.at[s], on_other(0))
         for o in OFFSETS:
 
             @pl.when(has(o))
@@ -264,20 +290,25 @@
                 near_copy(s, o).start()
 
         pl.when(s == 0)(prepare)
+        pl.when(s > 0)(lambda: wait_sends(s - 1))
 
         wait_blocks(tab_a.at[s], SIDE - 1, a_recv.at[s])
         wait_blocks(tab_o.at[s], SIDE, o_recv.at[s])
-        total = jnp.zeros((HALF, 128), f32)
-        for i in range(SIDE):
-            total = total + tab_a[s, i, HALF:E].astype(f32) + tab_o[s, i].astype(f32)
-        tab_r[s, x, my_b] = total.astype(bf16)
-        mine = tab_r.at[s, x, my_b]
-        for dx, d in far_xb:
-            push(mine, mine, r_send.at[s], r_recv.at[s], on_xb(dx, d))
+        row_sum = jnp.sum(tab_a[s, :, HALF:E].astype(f32) + tab_o[s].astype(f32), axis=0)
+        tab_p[s, my_b] = row_sum.astype(bf16)
+        mine = tab_p.at[s, my_b]
+        for d in FAR_FIRST:
+            push(mine, mine, p_send.at[s], p_recv.at[s], on_b(d))
         tab_b[s, my_b] = tab_a[s, :, 0:HALF]
         mine = tab_b.at[s, my_b]
         for d in FAR_FIRST:
             push(mine, mine, b_send.at[s], b_recv.at[s], on_b(d))
+
+        wait_blocks(tab_p.at[s], SIDE - 1, p_recv.at[s])
+        tab_x[s, x] = jnp.sum(tab_p[s].astype(f32), axis=0).astype(bf16)
+        mine = tab_x.at[s, x]
+        for d in X_FIRST:
+            push(mine, mine, x_send.at[s], x_recv.at[s], on_x(d))
 
         for o in OFFSETS:
 
@@ -308,7 +339,7 @@
         for c in range(CL):
             velocity = jnp.exp(u_now[c])
             ds = jnp.exp(-s_now[c]) - velocity
-            out[1, c] += weight * ds
+            s_sum[c] += weight * ds
             s_now[c] = s_in[c] + ahead * ds
             inverse[c] = 1.0 / (a_ref[c : c + 1] + viscous * velocity)
             known[c] = near[c * E : (c + 1) * E] + b_ref[c : c + 1] * ds
@@ -325,9 +356,9 @@
                 j = half * CL + c
                 known[c, half * HALF : (half + 1) * HALF] += far[:, j * PS : (j + 1) * PS]
 
-        wait_blocks(tab_r.at[s].reshape(XS * SIDE, HALF, 128), XS * SIDE - 1, r_recv.at[s])
+        wait_blocks(tab_x.at[s], XS - 1, x_recv.at[s])
         low = block < CL
-        sums = [jnp.sum(tab_r[s, i].astype(f32), axis=0) for i in range(XS)]
+        sums = [tab_x[s, i].astype(f32) for i in range(XS)]
         turned = [pltpu.roll(v, 64, 1) for v in sums]
         rows = []
         for half in range(2):
@@ -344,22 +375,18 @@
         for c in range(CL):
             du = -(known[c] + coarse_far[:, c * PS : (c + 1) * PS]) * inverse[c]
             u_now[c] = u_in[c] + ahead * du
-            out[0, c] += weight * du
-
-        wait_blocks(tab_a.at[s], SIDE - 1, a_send.at[s])
-        wait_blocks(tab_o.at[s], SIDE, o_send.at[s])
-        wait_blocks(tab_r.at[s].reshape(XS * SIDE, HALF, 128), XS * SIDE - 1, r_send.at[s])
-        wait_blocks(tab_b.at[s], SIDE - 1, b_send.at[s])
-        for o in OFFSETS:
-
-            @pl.when(has(o))
-            def _():
-                near_copy(s, o).wait_send()
-
+            u_sum[c] += weight * du
+
+        pl.when(s < STAGES - 1)(lambda: begin(s + 1))
         return carry
 
-    pl.semaphore_wait(barrier, XS * SIDE - 1 + 2 * SIDE - 1 + n_near)
+    begin(0)
+    pl.semaphore_wait(barrier, len(partners) + n_near)
     lax.fori_loop(0, STAGES, stage, 0)
+    wait_sends(STAGES - 1)
+    for c in range(CL):
+        out[0, :, c] = (time_step / 6.0) * u_sum[c]
+        out[1, :, c] = (time_step / 6.0) * s_sum[c]
 
 
 def per_device(
@@ -379,16 +406,20 @@
     coarse_coupling,
 ):
     vmem = pl.BlockSpec(memory_space=pltpu.VMEM)
-    smem = pl.BlockSpec(memory_space=pltpu.SMEM)
     hbm = pl.BlockSpec(memory_space=pl.ANY)
     state = (CL, E, PS)
     dma = pltpu.SemaphoreType.DMA
-    sums = pl.pallas_call(
+    step = pl.pallas_call(
         kernel,
-        out_shape=jax.ShapeDtypeStruct((2, *state), f32),
-        in_specs=[smem] * 5 + [hbm] * 9,
+        out_shape=jax.ShapeDtypeStruct((2, E, CL, PS), f32),
+        in_specs=[hbm] * 14,
         out_specs=vmem,
         scratch_shapes=[
+            pltpu.SMEM((1, NB), i32),
+            pltpu.SMEM((1, NB), i32),
+            pltpu.SMEM((1,), i32),
+            pltpu.SMEM((1, NF), i32),
+            pltpu.SMEM((1, NF), i32),
             pltpu.VMEM(state, f32),
             pltpu.VMEM(state, f32),
             pltpu.VMEM((CL, PS), f32),
@@ -409,16 +440,19 @@
             pltpu.VMEM(state, f32),
             pltpu.VMEM(state, f32),
             pltpu.VMEM(state, f32),
+            pltpu.VMEM(state, f32),
+            pltpu.VMEM(state, f32),
             pltpu.VMEM((STAGES, SIDE, E, 128), bf16),
             pltpu.VMEM((STAGES, SIDE, HALF, 128), bf16),
-            pltpu.VMEM((STAGES, XS, SIDE, HALF, 128), bf16),
+            pltpu.VMEM((STAGES, SIDE, HALF, 128), bf16),
+            pltpu.VMEM((STAGES, XS, HALF, 128), bf16),
             pltpu.VMEM((STAGES, SIDE, SIDE, HALF, 128), bf16),
             pltpu.VMEM((STAGES, (2 * REACH + 1) * CL, E, PS), bf16),
             pltpu.VMEM(((2 * REACH + 1) * CL, E, PS), bf16),
             pltpu.VMEM((SIDE * SIDE, HALF, 128), bf16),
-            dma((11,)),
+            dma((16,)),
         ]
-        + [dma((STAGES,))] * 8
+        + [dma((STAGES,))] * 10
         + [dma((STAGES, 2 * REACH + 1))] * 2,
         compiler_params=pltpu.CompilerParams(
             collective_id=0, has_side_effects=True, vmem_limit_bytes=56 * 1024 * 1024
@@ -439,8 +473,7 @@
         transfer,
         coarse_coupling,
     )
-    sums = (time_step / 6.0) * sums.transpose(0, 2, 1, 3)
-    return log_rate + sums[0], state_log + sums[1]
+    return log_rate + step[0], state_log + step[1]
 
 
 def solution(mesh):

time: 75.1 us -> 71.3 us (0.949)
  Pallas kernels: 71.2 us -> 68 us
  local copies, waits for them, and re-layouts: 1.37 us -> 0.01 us
    pallas_call x1, Pallas kernels: 71.2 us -> 68 us  [per_device(): pl.pallas_call(kernel, out_shape=jax.ShapeDtypeStruct((2, E, CL, PS), f32...]
    add x1, other arithmetic: 0.02 us -> 1.59 us  [per_device(): return (log_rate + step[0], state_log + step[1])]
    unnamed x6 -> x4, local copies, waits for them, and re-layouts: 1.37 us -> 0.01 us
    mul x1 -> x0, other arithmetic: 0.92 us -> none  [per_device(): sums = time_step / 6.0 * sums.transpose(0, 2, 1, 3)]
where the time goes in v3:
time: 71.3 us; the launch traced here: 71 us
  Pallas kernels  68 us (95%)
  other arithmetic  1.59 us (2%)
  between operations  1.35 us (2%)
    pallas_call x1, Pallas kernels, per_device(): pl.pallas_call(kernel, out_shape=jax.ShapeDtypeStruct((2, E, CL, PS), f32...  68 us
    add x1, other arithmetic, per_device(): return (log_rate + step[0], state_log + step[1])  1.59 us

profile of v3, /device:TPU:1, one launch (start us, length us, event | category | flops | bytes accessed | tf_op | source)
XLA Modules:
  0.0 71.0 jit_solution(10354133790487343476)
XLA Ops:
  0.6 0.0 copy-start
  0.6 0.0 copy-start.1
  1.3 68.0 %shard_map.149 = f32[2,32,2,256]{3,2,1,0:T(2,128)} custom-call(s32[1,32]{1,0:T(1,128)} %near_src_hbm.1, s32[1,32]{1,0:T(1,128)} %near_dst_hbm.1, s32[1]{0:T(128)S(6)} %copy.16.near_count_hbm, s32[1,32]{1,0:T(1,128)} %far_src_hbm.1, s32[1,32]{1,0:T(1,128)} %far_dst_hbm.1, f32[32,2,256]{2,1,0:T(2,128)} %u_hbm.1, f32[32,2,256]{2,1,0:T(2,128)} %s_hbm.1, ...), custom_call_target="tpu_custom_call" | custom-call | tf_op jit(solution)/shard_map/pallas_call | solution.py:412
  69.4 0.0 copy-done
  69.4 0.0 copy-done.1
  69.4 1.6 %bitcast_add_fusion = (f32[32,2,256]{2,1,0:T(2,128)}, f32[32,2,256]{2,1,0:T(2,128)}) fusion(f32[32,2,256]{2,1,0:T(2,128)S(1)} %copy-done, f32[2,32,2,256]{3,2,1,0:T(2,128)} %shard_map.149, f32[32,2,256]{2,1,0:T(2,128)S(1)} %copy-done.1), kind=kLoop, calls=%fused_computation | loop fusion | flops 32768 | bytes 393216 | tf_op jit(solution)/shard_map/add | solution.py:476
Async XLA Ops:
  0.6 68.7 %copy-start = (f32[32,2,256]{2,1,0:T(2,128)S(1)}, f32[32,2,256]{2,1,0:T(2,128)}, u32[]{:S(2)}) copy-start(f32[32,2,256]{2,1,0:T(2,128)} %s_hbm.1) | copy-start | bytes 196612
  0.6 68.7 %copy-start.1 = (f32[32,2,256]{2,1,0:T(2,128)S(1)}, f32[32,2,256]{2,1,0:T(2,128)}, u32[]{:S(2)}) copy-start(f32[32,2,256]{2,1,0:T(2,128)} %u_hbm.1) | copy-start | bytes 196612

commit v4 on v3

--- a/solution.py
+++ b/solution.py
@@ -27,8 +27,12 @@
 i32 = jnp.int32
 
 FAR_FIRST = (4, 3, 5, 2, 6, 1, 7)
-X_FIRST = (2, 1, 3)
+FIRST = 12
 OFFSETS = (-2, 2, -1, 1)
+
+
+def ring(d, size):
+    return min(d, size - d)
 
 
 def split(x):
@@ -59,24 +63,26 @@
     near_src,
     near_dst,
     near_count,
-    far_src,
-    far_dst,
     u_in,
     s_in,
     a_ref,
     b_ref,
     blocks,
+    far_src_row,
+    far_dst_row,
     coupling,
     bases,
     transfer,
     coarse,
     near_at,
     near_to,
-    far_at,
     w_coefs,
+    w_built,
+    w_sent,
+    w_came,
+    w_own,
     w_far,
-    w_coarse,
-    w_bases,
+    w_sum,
     u_now,
     s_now,
     inverse,
@@ -85,23 +91,27 @@
     s_sum,
     tab_a,
     tab_o,
-    tab_p,
-    tab_x,
+    tab_r,
     tab_b,
+    tab_f,
+    part_f,
+    expansion,
     tab_n,
     work_n,
-    work_b,
     load_sem,
+    coupling_sem,
     a_send,
     a_recv,
     o_send,
     o_recv,
-    p_send,
-    p_recv,
-    x_send,
-    x_recv,
+    r_send,
+    r_recv,
+    f_send,
+    f_recv,
     b_send,
     b_recv,
+    w_send,
+    w_recv,
     n_send,
     n_recv,
 ):
@@ -129,14 +139,19 @@
     def from_other(d):
         return (other, lax.rem(my_a + d, SIDE) * step_a + my_b * step_b)
 
-    def on_x(d):
-        return (lax.rem(x + d, XS) * 2 + core, dv)
+    def on_xb(dx, d):
+        return (lax.rem(x + dx, XS) * 2 + core, my_a * step_a + lax.rem(my_b + d, SIDE) * step_b)
+
+    far_xb = sorted(
+        ((dx, d) for dx in range(XS) for d in range(SIDE) if dx or d),
+        key=lambda p: -(ring(p[0], XS) + ring(p[1], SIDE)),
+    )
 
     def has(o):
         return (dv + o >= 0) & (dv + o < SIDE * SIDE)
 
-    partners = [to(d) for d in FAR_FIRST for to in (on_a, from_other, on_b)] + [from_other(0)]
-    partners += [on_x(d) for d in X_FIRST]
+    partners = [on_xb(dx, d) for dx, d in far_xb]
+    partners += [to(d) for d in FAR_FIRST for to in (on_a, from_other)] + [from_other(0)]
     barrier = pltpu.get_barrier_semaphore()
     for to in partners:
         pl.semaphore_signal(barrier, inc=1, device_id=to)
@@ -156,18 +171,21 @@
         (near_src_hbm, near_src),
         (near_dst_hbm, near_dst),
         (near_count_hbm, near_count),
-        (far_src_hbm, far_src),
-        (far_dst_hbm, far_dst),
+        (far_src_hbm, far_src_row),
+        (far_dst_hbm, far_dst_row),
         (s_hbm.at[:, 0], s_in.at[0]),
         (s_hbm.at[:, 1], s_in.at[1]),
         (a_hbm, a_ref),
         (b_hbm, b_ref),
-        (coupling_hbm.at[0], coupling),
         (coarse_hbm, coarse),
         (blocks_hbm.at[0], blocks),
     ]
     loads = [pltpu.make_async_copy(src, dst, load_sem.at[i]) for i, (src, dst) in enumerate(loads)]
-    for load in loads:
+    for load in loads[:4]:
+        load.start()
+    for r in range(R):
+        pltpu.make_async_copy(coupling_hbm.at[0, :, r], coupling.at[r], coupling_sem).start()
+    for load in loads[4:]:
         load.start()
 
     for o in OFFSETS:
@@ -194,8 +212,65 @@
     u_sum[...] = jnp.zeros_like(u_sum)
     s_sum[...] = jnp.zeros_like(s_sum)
 
+    def build_far():
+        for load in loads[4:9]:
+            load.wait()
+        pltpu.make_async_copy(coupling, coupling, coupling_sem).wait()
+        src = far_src_row[...]
+        owner = src >> 1
+        its_y, its_z = owner & (SIDE - 1), owner >> 3
+        its_a, its_b = its_y + core * (its_z - its_y), its_z + core * (its_y - its_z)
+        place = jnp.concatenate([its_b * SIDE + its_a] * 4, axis=1)
+        kind = jnp.concatenate([(src & 1) * CL + far_dst_row[...]] * 4, axis=1)
+        places = SIDE * SIDE
+        chosen = (lax.broadcasted_iota(i32, (places, 128), 0) == place) & (lane_block(places) == kind)
+        chosen = jnp.where(chosen, 1.0, 0.0).astype(bf16)
+        chosen = jnp.concatenate([chosen, chosen], axis=1)
+        quarter = lane_block(NF)
+
+        def rows_of(r4, carry):
+            for i in range(4):
+                r = r4 * 4 + i
+                wide = jnp.concatenate([coupling[r]] * 4, axis=1)
+                parts = [split(jnp.where(quarter == j, wide, 0.0)) for j in range(4)]
+                right = jnp.concatenate([p[0] for p in parts] + [p[1] for p in parts], axis=0)
+                rows = jnp.dot(chosen, right, preferred_element_type=f32)
+                at = pl.ds(pl.multiple_of(r * SIDE, SIDE), SIDE)
+                w_built[:, at] = rows.reshape(SIDE, SIDE, 128)
+            return carry
+
+        lax.fori_loop(0, R // 4, rows_of, 0)
+        for b in range(SIDE):
+            for a in range(SIDE):
+                w_sent[b, a] = w_built[b, pl.ds(a, R, stride=SIDE), :].astype(bf16)
+        w_came[my_b] = w_sent[my_b]
+
+        def unpack_own(b, carry):
+            unpack(w_sent, b, lambda a, j: w_own.at[pl.ds(pl.multiple_of(b * SIDE * 128 + a * 128 + j * R, R), R)])
+            return carry
+
+        lax.fori_loop(0, SIDE, unpack_own, 0)
+
+    def unpack(packed, b, to):
+        low = lax.broadcasted_iota(i32, (R, 128), 1) < 64
+        for a in range(SIDE):
+            block = packed[b, a].astype(f32)
+            turned = pltpu.roll(block, 64, 1)
+            for j, (here, mask) in enumerate(((block, low), (turned, low), (turned, ~low), (block, ~low))):
+                to(a, j)[...] = jnp.where(mask, here, 0.0).astype(bf16)
+
+    def unpack_far():
+        wait_blocks(w_came, SIDE - 1, w_recv)
+
+        def column_of(b, carry):
+            at = pl.ds(pl.multiple_of(b * 128, 128), 128)
+            unpack(w_came, b, lambda a, j: w_far.at[pl.ds(a * 128 + j * R, R), at])
+            return carry
+
+        lax.fori_loop(0, SIDE, column_of, 0)
+
     def prepare():
-        for load in loads[4:]:
+        for load in loads[9:]:
             load.wait()
         count = near_count[0]
         for k in range(NB):
@@ -204,10 +279,6 @@
             near_at[k] = jnp.minimum(jnp.maximum(at, 0), (2 * REACH + 1) * CL - 1)
             for c in range(CL):
                 near_to[c, k] = jnp.where((near_dst[0, k] == c) & (count > k), 1.0, 0.0).astype(f32)
-        for k in range(NF):
-            owner = lax.div(far_src[0, k], CL)
-            turned = lax.rem(owner, SIDE) * SIDE + lax.div(owner, SIDE)
-            far_at[k] = owner + core * (turned - owner)
         for c in range(CL):
             s_now[c] = s_in[c]
             hi, lo = split(
@@ -215,23 +286,12 @@
                     coarse[c].reshape(GROUPS * R, R), bases[c].astype(f32), precision=highest, preferred_element_type=f32
                 )
             )
-            w_coarse[0 : GROUPS * R, c * PS : (c + 1) * PS] = hi
-            w_coarse[GROUPS * R :, c * PS : (c + 1) * PS] = lo
-        w_bases[...] = jnp.zeros_like(w_bases)
-        for half in range(2):
-            for c in range(CL):
-                j = half * CL + c
-                w_bases[j * R : (j + 1) * R, j * PS : (j + 1) * PS] = bases[c]
-        wide_block = lane_block(R)
-        for k in range(NF):
-            wide = jnp.concatenate([coupling[k]] * 4, axis=1)
-            for half in range(2):
-                for c in range(CL):
-                    lanes = jnp.where(lax.rem(far_src[0, k], CL) == c, half * CL + far_dst[0, k], -1)
-                    hi, lo = split(jnp.where(wide_block == lanes, wide, 0.0))
-                    at = k * 128 + (half * CL + c) * R
-                    w_far[0, at : at + R] = hi
-                    w_far[1, at : at + R] = lo
+            w_sum[0 : GROUPS * R, c * PS : (c + 1) * PS] = hi
+            w_sum[GROUPS * R : 2 * GROUPS * R, c * PS : (c + 1) * PS] = lo
+        w_sum[2 * GROUPS * R :] = jnp.zeros((128, CL * PS), bf16)
+        for c in range(CL):
+            at = 2 * GROUPS * R + c * R
+            w_sum[at : at + R, c * PS : (c + 1) * PS] = bases[c]
 
     def near_copy(s, o):
         return pltpu.make_async_remote_copy(
@@ -267,14 +327,37 @@
     def wait_sends(s):
         wait_blocks(tab_a.at[s], SIDE - 1, a_send.at[s])
         wait_blocks(tab_o.at[s], SIDE, o_send.at[s])
-        wait_blocks(tab_p.at[s], SIDE - 1, p_send.at[s])
-        wait_blocks(tab_x.at[s], XS - 1, x_send.at[s])
-        wait_blocks(tab_b.at[s], SIDE - 1, b_send.at[s])
+        wait_blocks(tab_r.at[s].reshape(XS * SIDE, HALF, 128), XS * SIDE - 1, r_send.at[s])
         for o in OFFSETS:
 
             @pl.when(has(o))
             def _():
                 near_copy(s, o).wait_send()
+
+    def send_first():
+        tab_b[my_b] = tab_a[0, :, 0:HALF]
+        for d in FAR_FIRST:
+            push(tab_b.at[my_b], tab_b.at[my_b], b_send, b_recv, on_b(d))
+        for d in FAR_FIRST:
+            push(w_sent.at[lax.rem(my_b + d, SIDE)], w_came.at[my_b], w_send, w_recv, on_b(d))
+
+    def far_first():
+        wait_blocks(tab_b, SIDE - 1, b_recv)
+        sources = jnp.concatenate([tab_b[b, a] for b in range(SIDE) for a in range(SIDE)], axis=1)
+        expansion[...] = jnp.dot(sources, w_own[...], preferred_element_type=f32)
+
+    def far_later(s):
+        wait_blocks(tab_f.at[s], SIDE - 1, f_recv.at[s])
+        expansion[...] = jnp.sum(tab_f[s].astype(f32), axis=0)
+
+    def send_far(s):
+        sources = jnp.concatenate([tab_a[s, i, 0:HALF] for i in range(SIDE)], axis=1)
+        parts = jnp.dot(sources, w_far[...], preferred_element_type=f32).astype(bf16)
+        for i in range(SIDE):
+            part_f[s, i] = parts[:, i * 128 : (i + 1) * 128]
+        for d in FAR_FIRST:
+            push(part_f.at[s, lax.rem(my_b + d, SIDE)], tab_f.at[s, my_b], f_send.at[s], f_recv.at[s], on_b(d))
+        tab_f[s, my_b] = part_f[s, my_b]
 
     def stage(s, carry):
         mine = tab_a.at[s, my_a]
@@ -289,26 +372,23 @@
             def _():
                 near_copy(s, o).start()
 
+        pl.when(s == 0)(build_far)
         pl.when(s == 0)(prepare)
+        pl.when(s == 1)(unpack_far)
         pl.when(s > 0)(lambda: wait_sends(s - 1))
 
         wait_blocks(tab_a.at[s], SIDE - 1, a_recv.at[s])
         wait_blocks(tab_o.at[s], SIDE, o_recv.at[s])
         row_sum = jnp.sum(tab_a[s, :, HALF:E].astype(f32) + tab_o[s].astype(f32), axis=0)
-        tab_p[s, my_b] = row_sum.astype(bf16)
-        mine = tab_p.at[s, my_b]
-        for d in FAR_FIRST:
-            push(mine, mine, p_send.at[s], p_recv.at[s], on_b(d))
-        tab_b[s, my_b] = tab_a[s, :, 0:HALF]
-        mine = tab_b.at[s, my_b]
-        for d in FAR_FIRST:
-            push(mine, mine, b_send.at[s], b_recv.at[s], on_b(d))
-
-        wait_blocks(tab_p.at[s], SIDE - 1, p_recv.at[s])
-        tab_x[s, x] = jnp.sum(tab_p[s].astype(f32), axis=0).astype(bf16)
-        mine = tab_x.at[s, x]
-        for d in X_FIRST:
-            push(mine, mine, x_send.at[s], x_recv.at[s], on_x(d))
+        tab_r[s, x, my_b] = row_sum.astype(bf16)
+        mine = tab_r.at[s, x, my_b]
+        for dx, d in far_xb[:FIRST]:
+            push(mine, mine, r_send.at[s], r_recv.at[s], on_xb(dx, d))
+        pl.when(s > 0)(lambda: send_far(s))
+        for dx, d in far_xb[FIRST:]:
+            push(mine, mine, r_send.at[s], r_recv.at[s], on_xb(dx, d))
+
+        pl.when(s == 0)(send_first)
 
         for o in OFFSETS:
 
@@ -344,21 +424,12 @@
             inverse[c] = 1.0 / (a_ref[c : c + 1] + viscous * velocity)
             known[c] = near[c * E : (c + 1) * E] + b_ref[c : c + 1] * ds
 
-        wait_blocks(tab_b.at[s], SIDE - 1, b_recv.at[s])
-        work_b[...] = tab_b[s].reshape(SIDE * SIDE, HALF, 128)
-        sources = jnp.concatenate([work_b[far_at[k]] for k in range(NF)], axis=1)
-        expansion = jnp.dot(sources, w_far[0], preferred_element_type=f32) + jnp.dot(
-            sources, w_far[1], preferred_element_type=f32
-        )
-        far = jnp.dot(expansion.astype(bf16), w_bases[...], preferred_element_type=f32)
-        for c in range(CL):
-            for half in range(2):
-                j = half * CL + c
-                known[c, half * HALF : (half + 1) * HALF] += far[:, j * PS : (j + 1) * PS]
-
-        wait_blocks(tab_x.at[s], XS - 1, x_recv.at[s])
+        pl.when(s == 0)(far_first)
+        pl.when(s > 0)(lambda: far_later(s))
+        halves = jnp.concatenate([expansion[...], pltpu.roll(expansion[...], 64, 1)], axis=0).astype(bf16)
+        wait_blocks(tab_r.at[s].reshape(XS * SIDE, HALF, 128), XS * SIDE - 1, r_recv.at[s])
         low = block < CL
-        sums = [tab_x[s, i].astype(f32) for i in range(XS)]
+        sums = [jnp.sum(tab_r[s, i].astype(f32), axis=0) for i in range(XS)]
         turned = [pltpu.roll(v, 64, 1) for v in sums]
         rows = []
         for half in range(2):
@@ -369,11 +440,11 @@
                 )
             )
         groups = jnp.concatenate(rows, axis=0).astype(bf16)
-        coarse_far = jnp.dot(
-            jnp.concatenate([groups, groups], axis=1), w_coarse[...], preferred_element_type=f32
+        far = jnp.dot(
+            jnp.concatenate([groups, groups, halves], axis=1), w_sum[...], preferred_element_type=f32
         )
         for c in range(CL):
-            du = -(known[c] + coarse_far[:, c * PS : (c + 1) * PS]) * inverse[c]
+            du = -(known[c] + far[:, c * PS : (c + 1) * PS]) * inverse[c]
             u_now[c] = u_in[c] + ahead * du
             u_sum[c] += weight * du
 
@@ -384,6 +455,10 @@
     pl.semaphore_wait(barrier, len(partners) + n_near)
     lax.fori_loop(0, STAGES, stage, 0)
     wait_sends(STAGES - 1)
+    wait_blocks(tab_b, SIDE - 1, b_send)
+    wait_blocks(w_came, SIDE - 1, w_send)
+    for s in range(1, STAGES):
+        wait_blocks(tab_f.at[s], SIDE - 1, f_send.at[s])
     for c in range(CL):
         out[0, :, c] = (time_step / 6.0) * u_sum[c]
         out[1, :, c] = (time_step / 6.0) * s_sum[c]
@@ -418,24 +493,26 @@
             pltpu.SMEM((1, NB), i32),
             pltpu.SMEM((1, NB), i32),
             pltpu.SMEM((1,), i32),
-            pltpu.SMEM((1, NF), i32),
-            pltpu.SMEM((1, NF), i32),
             pltpu.VMEM(state, f32),
             pltpu.VMEM(state, f32),
             pltpu.VMEM((CL, PS), f32),
             pltpu.VMEM((CL, PS), f32),
             pltpu.VMEM((NB, PS, PS), bf16),
-            pltpu.VMEM((NF, R, R), f32),
+            pltpu.VMEM((1, NF), i32),
+            pltpu.VMEM((1, NF), i32),
+            pltpu.VMEM((R, NF, R), f32),
             pltpu.VMEM((CL, R, PS), bf16),
             pltpu.VMEM((CL, R, R), f32),
             pltpu.VMEM((CL, GROUPS, R, R), f32),
             pltpu.SMEM((NB,), i32),
             pltpu.SMEM((CL, NB), f32),
-            pltpu.SMEM((NF,), i32),
             pltpu.VMEM((CL * PS, 256), bf16),
-            pltpu.VMEM((2, NF * 128, 128), bf16),
-            pltpu.VMEM((2 * GROUPS * R, CL * PS), bf16),
-            pltpu.VMEM((2 * CL * R, 2 * CL * PS), bf16),
+            pltpu.VMEM((SIDE, R * SIDE, 128), f32),
+            pltpu.VMEM((SIDE, SIDE, R, 128), bf16),
+            pltpu.VMEM((SIDE, SIDE, R, 128), bf16),
+            pltpu.VMEM((SIDE * SIDE * 128, 128), bf16),
+            pltpu.VMEM((SIDE * 128, SIDE * 128), bf16),
+            pltpu.VMEM((2 * GROUPS * R + 128, CL * PS), bf16),
             pltpu.VMEM(state, f32),
             pltpu.VMEM(state, f32),
             pltpu.VMEM(state, f32),
@@ -444,15 +521,18 @@
             pltpu.VMEM(state, f32),
             pltpu.VMEM((STAGES, SIDE, E, 128), bf16),
             pltpu.VMEM((STAGES, SIDE, HALF, 128), bf16),
+            pltpu.VMEM((STAGES, XS, SIDE, HALF, 128), bf16),
+            pltpu.VMEM((SIDE, SIDE, HALF, 128), bf16),
             pltpu.VMEM((STAGES, SIDE, HALF, 128), bf16),
-            pltpu.VMEM((STAGES, XS, HALF, 128), bf16),
-            pltpu.VMEM((STAGES, SIDE, SIDE, HALF, 128), bf16),
+            pltpu.VMEM((STAGES, SIDE, HALF, 128), bf16),
+            pltpu.VMEM((HALF, 128), f32),
             pltpu.VMEM((STAGES, (2 * REACH + 1) * CL, E, PS), bf16),
             pltpu.VMEM(((2 * REACH + 1) * CL, E, PS), bf16),
-            pltpu.VMEM((SIDE * SIDE, HALF, 128), bf16),
-            dma((16,)),
+            dma((15,)),
+            dma,
         ]
-        + [dma((STAGES,))] * 10
+        + [dma((STAGES,))] * 8
+        + [dma] * 4
         + [dma((STAGES, 2 * REACH + 1))] * 2,
         compiler_params=pltpu.CompilerParams(
             collective_id=0, has_side_effects=True, vmem_limit_bytes=56 * 1024 * 1024

time: 71.3 us -> 69.6 us (0.976)
  Pallas kernels: 68 us -> 66.4 us
    pallas_call x1, Pallas kernels: 68 us -> 66.4 us  [per_device(): pl.pallas_call(kernel, out_shape=jax.ShapeDtypeStruct((2, E, CL, PS), f32...]
where the time goes in v4:
time: 69.6 us; the launch traced here: 69.4 us
  Pallas kernels  66.4 us (95%)
  other arithmetic  1.59 us (2%)
  between operations  1.35 us (2%)
    pallas_call x1, Pallas kernels, per_device(): pl.pallas_call(kernel, out_shape=jax.ShapeDtypeStruct((2, E, CL, PS), f32...  66.4 us
    add x1, other arithmetic, per_device(): return (log_rate + step[0], state_log + step[1])  1.59 us

profile of v4, /device:TPU:1, one launch (start us, length us, event | category | flops | bytes accessed | tf_op | source)
XLA Modules:
  0.0 69.4 jit_solution(2928875555656110115)
XLA Ops:
  0.6 0.0 copy-start
  0.6 0.0 copy-start.1
  1.3 66.4 %shard_map.149 = f32[2,32,2,256]{3,2,1,0:T(2,128)} custom-call(s32[1,32]{1,0:T(1,128)} %near_src_hbm.1, s32[1,32]{1,0:T(1,128)} %near_dst_hbm.1, s32[1]{0:T(128)S(6)} %copy.16.near_count_hbm, s32[1,32]{1,0:T(1,128)} %far_src_hbm.1, s32[1,32]{1,0:T(1,128)} %far_dst_hbm.1, f32[32,2,256]{2,1,0:T(2,128)} %u_hbm.1, f32[32,2,256]{2,1,0:T(2,128)} %s_hbm.1, ...), custom_call_target="tpu_custom_call" | custom-call | tf_op jit(solution)/shard_map/pallas_call | solution.py:487
  67.8 0.0 copy-done
  67.8 0.0 copy-done.1
  67.8 1.6 %bitcast_add_fusion = (f32[32,2,256]{2,1,0:T(2,128)}, f32[32,2,256]{2,1,0:T(2,128)}) fusion(f32[32,2,256]{2,1,0:T(2,128)S(1)} %copy-done, f32[2,32,2,256]{3,2,1,0:T(2,128)} %shard_map.149, f32[32,2,256]{2,1,0:T(2,128)S(1)} %copy-done.1), kind=kLoop, calls=%fused_computation | loop fusion | flops 32768 | bytes 393216 | tf_op jit(solution)/shard_map/add | solution.py:556
Async XLA Ops:
  0.6 67.1 %copy-start = (f32[32,2,256]{2,1,0:T(2,128)S(1)}, f32[32,2,256]{2,1,0:T(2,128)}, u32[]{:S(2)}) copy-start(f32[32,2,256]{2,1,0:T(2,128)} %s_hbm.1) | copy-start | bytes 196612
  0.6 67.1 %copy-start.1 = (f32[32,2,256]{2,1,0:T(2,128)S(1)}, f32[32,2,256]{2,1,0:T(2,128)}, u32[]{:S(2)}) copy-start(f32[32,2,256]{2,1,0:T(2,128)} %u_hbm.1) | copy-start | bytes 196612

commit v5 on v4

--- a/solution.py
+++ b/solution.py
@@ -150,19 +150,6 @@
     def has(o):
         return (dv + o >= 0) & (dv + o < SIDE * SIDE)
 
-    partners = [on_xb(dx, d) for dx, d in far_xb]
-    partners += [to(d) for d in FAR_FIRST for to in (on_a, from_other)] + [from_other(0)]
-    barrier = pltpu.get_barrier_semaphore()
-    for to in partners:
-        pl.semaphore_signal(barrier, inc=1, device_id=to)
-    n_near = jnp.int32(0)
-    for o in OFFSETS:
-        n_near = n_near + has(o).astype(i32)
-
-        @pl.when(has(o))
-        def _():
-            pl.semaphore_signal(barrier, inc=1, device_id=(st, dv + o))
-
     loads = [
         (u_hbm.at[:, 0], u_in.at[0]),
         (u_hbm.at[:, 1], u_in.at[1]),
@@ -183,6 +170,19 @@
     loads = [pltpu.make_async_copy(src, dst, load_sem.at[i]) for i, (src, dst) in enumerate(loads)]
     for load in loads[:4]:
         load.start()
+    partners = [to(d) for d in FAR_FIRST for to in (on_a, from_other)] + [from_other(0)]
+    partners += [on_xb(dx, d) for dx, d in far_xb]
+    barrier = pltpu.get_barrier_semaphore()
+    for to in partners:
+        pl.semaphore_signal(barrier, inc=1, device_id=to)
+    n_near = jnp.int32(0)
+    for o in OFFSETS:
+        n_near = n_near + has(o).astype(i32)
+
+        @pl.when(has(o))
+        def _():
+            pl.semaphore_signal(barrier, inc=1, device_id=(st, dv + o))
+
     for r in range(R):
         pltpu.make_async_copy(coupling_hbm.at[0, :, r], coupling.at[r], coupling_sem).start()
     for load in loads[4:]:
@@ -203,9 +203,13 @@
         lane = lax.broadcasted_iota(i32, (R, 128), 1)
         placed = ((lane % R == row) & ((lane // R) % CL == c)).astype(f32)
         right = jnp.concatenate([placed] + [transfer[c]] * 4, axis=1)
-        w_coefs[c * PS : (c + 1) * PS] = lax.dot_general(
-            bases[c].astype(f32), right, (((0,), (0,)), ((), ())), precision=highest, preferred_element_type=f32
-        ).astype(bf16)
+        hi, lo = split(
+            lax.dot_general(
+                bases[c].astype(f32), right, (((0,), (0,)), ((), ())), precision=highest, preferred_element_type=f32
+            )
+        )
+        w_coefs[c * PS : (c + 1) * PS, 0:256] = hi
+        w_coefs[c * PS : (c + 1) * PS, 256:384] = lo[:, 128:256]
 
     for c in range(CL):
         u_now[c] = u_in[c]
@@ -319,8 +323,9 @@
         deficit = jnp.concatenate([tab_n[s, REACH * CL + c] for c in range(CL)], axis=1)
         both = jnp.dot(deficit, w_coefs[...], preferred_element_type=f32)
         coefs = jnp.where(block < CL, both[0:HALF, 0:128], both[HALF:E, 0:128])
-        share = jnp.where(block == core, both[0:HALF, 128:256], 0.0)
-        share = jnp.where(block == CL + core, both[HALF:E, 128:256], share)
+        shares = both[:, 128:256] + both[:, 256:384]
+        share = jnp.where(block == core, shares[0:HALF], 0.0)
+        share = jnp.where(block == CL + core, shares[HALF:E], share)
         tab_a[s, my_a, 0:HALF] = coefs.astype(bf16)
         tab_a[s, my_a, HALF:E] = share.astype(bf16)
 
@@ -334,10 +339,12 @@
             def _():
                 near_copy(s, o).wait_send()
 
-    def send_first():
+    def send_coefs():
         tab_b[my_b] = tab_a[0, :, 0:HALF]
         for d in FAR_FIRST:
             push(tab_b.at[my_b], tab_b.at[my_b], b_send, b_recv, on_b(d))
+
+    def send_weights():
         for d in FAR_FIRST:
             push(w_sent.at[lax.rem(my_b + d, SIDE)], w_came.at[my_b], w_send, w_recv, on_b(d))
 
@@ -384,11 +391,12 @@
         mine = tab_r.at[s, x, my_b]
         for dx, d in far_xb[:FIRST]:
             push(mine, mine, r_send.at[s], r_recv.at[s], on_xb(dx, d))
+        pl.when(s == 0)(send_coefs)
         pl.when(s > 0)(lambda: send_far(s))
         for dx, d in far_xb[FIRST:]:
             push(mine, mine, r_send.at[s], r_recv.at[s], on_xb(dx, d))
 
-        pl.when(s == 0)(send_first)
+        pl.when(s == 0)(send_weights)
 
         for o in OFFSETS:
 
@@ -506,7 +514,7 @@
             pltpu.VMEM((CL, GROUPS, R, R), f32),
             pltpu.SMEM((NB,), i32),
             pltpu.SMEM((CL, NB), f32),
-            pltpu.VMEM((CL * PS, 256), bf16),
+            pltpu.VMEM((CL * PS, 384), bf16),
             pltpu.VMEM((SIDE, R * SIDE, 128), f32),
             pltpu.VMEM((SIDE, SIDE, R, 128), bf16),
             pltpu.VMEM((SIDE, SIDE, R, 128), bf16),

time: 69.6 us -> 70 us (level)
  no operation moved by 1% of the time
where the time goes in v5:
time: 70 us; the launch traced here: 69.8 us
  Pallas kernels  66.8 us (95%)
  other arithmetic  1.59 us (2%)
  between operations  1.35 us (2%)
    pallas_call x1, Pallas kernels, per_device(): pl.pallas_call(kernel, out_shape=jax.ShapeDtypeStruct((2, E, CL, PS), f32...  66.8 us
    add x1, other arithmetic, per_device(): return (log_rate + step[0], state_log + step[1])  1.59 us

profile of v5, /device:TPU:1, one launch (start us, length us, event | category | flops | bytes accessed | tf_op | source)
XLA Modules:
  0.0 69.8 jit_solution(17682352346566158916)
XLA Ops:
  0.6 0.0 copy-start
  0.6 0.0 copy-start.1
  1.3 66.8 %shard_map.149 = f32[2,32,2,256]{3,2,1,0:T(2,128)} custom-call(s32[1,32]{1,0:T(1,128)} %near_src_hbm.1, s32[1,32]{1,0:T(1,128)} %near_dst_hbm.1, s32[1]{0:T(128)S(6)} %copy.16.near_count_hbm, s32[1,32]{1,0:T(1,128)} %far_src_hbm.1, s32[1,32]{1,0:T(1,128)} %far_dst_hbm.1, f32[32,2,256]{2,1,0:T(2,128)} %u_hbm.1, f32[32,2,256]{2,1,0:T(2,128)} %s_hbm.1, ...), custom_call_target="tpu_custom_call" | custom-call | tf_op jit(solution)/shard_map/pallas_call | solution.py:495
  68.2 0.0 copy-done
  68.2 0.0 copy-done.1
  68.2 1.6 %bitcast_add_fusion = (f32[32,2,256]{2,1,0:T(2,128)}, f32[32,2,256]{2,1,0:T(2,128)}) fusion(f32[32,2,256]{2,1,0:T(2,128)S(1)} %copy-done, f32[2,32,2,256]{3,2,1,0:T(2,128)} %shard_map.149, f32[32,2,256]{2,1,0:T(2,128)S(1)} %copy-done.1), kind=kLoop, calls=%fused_computation | loop fusion | flops 32768 | bytes 393216 | tf_op jit(solution)/shard_map/add | solution.py:564
Async XLA Ops:
  0.6 67.5 %copy-start = (f32[32,2,256]{2,1,0:T(2,128)S(1)}, f32[32,2,256]{2,1,0:T(2,128)}, u32[]{:S(2)}) copy-start(f32[32,2,256]{2,1,0:T(2,128)} %s_hbm.1) | copy-start | bytes 196612
  0.6 67.5 %copy-start.1 = (f32[32,2,256]{2,1,0:T(2,128)S(1)}, f32[32,2,256]{2,1,0:T(2,128)}, u32[]{:S(2)}) copy-start(f32[32,2,256]{2,1,0:T(2,128)} %u_hbm.1) | copy-start | bytes 196612

commit v6 on v4

--- a/solution.py
+++ b/solution.py
@@ -203,9 +203,13 @@
         lane = lax.broadcasted_iota(i32, (R, 128), 1)
         placed = ((lane % R == row) & ((lane // R) % CL == c)).astype(f32)
         right = jnp.concatenate([placed] + [transfer[c]] * 4, axis=1)
-        w_coefs[c * PS : (c + 1) * PS] = lax.dot_general(
-            bases[c].astype(f32), right, (((0,), (0,)), ((), ())), precision=highest, preferred_element_type=f32
-        ).astype(bf16)
+        hi, lo = split(
+            lax.dot_general(
+                bases[c].astype(f32), right, (((0,), (0,)), ((), ())), precision=highest, preferred_element_type=f32
+            )
+        )
+        w_coefs[c * PS : (c + 1) * PS, 0:256] = hi
+        w_coefs[c * PS : (c + 1) * PS, 256:384] = lo[:, 128:256]
 
     for c in range(CL):
         u_now[c] = u_in[c]
@@ -319,8 +323,9 @@
         deficit = jnp.concatenate([tab_n[s, REACH * CL + c] for c in range(CL)], axis=1)
         both = jnp.dot(deficit, w_coefs[...], preferred_element_type=f32)
         coefs = jnp.where(block < CL, both[0:HALF, 0:128], both[HALF:E, 0:128])
-        share = jnp.where(block == core, both[0:HALF, 128:256], 0.0)
-        share = jnp.where(block == CL + core, both[HALF:E, 128:256], share)
+        shares = both[:, 128:256] + both[:, 256:384]
+        share = jnp.where(block == core, shares[0:HALF], 0.0)
+        share = jnp.where(block == CL + core, shares[HALF:E], share)
         tab_a[s, my_a, 0:HALF] = coefs.astype(bf16)
         tab_a[s, my_a, HALF:E] = share.astype(bf16)
 
@@ -506,7 +511,7 @@
             pltpu.VMEM((CL, GROUPS, R, R), f32),
             pltpu.SMEM((NB,), i32),
             pltpu.SMEM((CL, NB), f32),
-            pltpu.VMEM((CL * PS, 256), bf16),
+            pltpu.VMEM((CL * PS, 384), bf16),
             pltpu.VMEM((SIDE, R * SIDE, 128), f32),
             pltpu.VMEM((SIDE, SIDE, R, 128), bf16),
             pltpu.VMEM((SIDE, SIDE, R, 128), bf16),

time: 69.6 us -> 69.6 us (level)
  no operation moved by 1% of the time
where the time goes in v6:
time: 69.6 us; the launch traced here: 69.4 us
  Pallas kernels  66.4 us (95%)
  other arithmetic  1.59 us (2%)
  between operations  1.35 us (2%)
    pallas_call x1, Pallas kernels, per_device(): pl.pallas_call(kernel, out_shape=jax.ShapeDtypeStruct((2, E, CL, PS), f32...  66.4 us
    add x1, other arithmetic, per_device(): return (log_rate + step[0], state_log + step[1])  1.59 us

profile of v6, /device:TPU:1, one launch (start us, length us, event | category | flops | bytes accessed | tf_op | source)
XLA Modules:
  0.0 69.4 jit_solution(12992847420167372498)
XLA Ops:
  0.6 0.0 copy-start
  0.6 0.0 copy-start.1
  1.3 66.4 %shard_map.149 = f32[2,32,2,256]{3,2,1,0:T(2,128)} custom-call(s32[1,32]{1,0:T(1,128)} %near_src_hbm.1, s32[1,32]{1,0:T(1,128)} %near_dst_hbm.1, s32[1]{0:T(128)S(6)} %copy.16.near_count_hbm, s32[1,32]{1,0:T(1,128)} %far_src_hbm.1, s32[1,32]{1,0:T(1,128)} %far_dst_hbm.1, f32[32,2,256]{2,1,0:T(2,128)} %u_hbm.1, f32[32,2,256]{2,1,0:T(2,128)} %s_hbm.1, ...), custom_call_target="tpu_custom_call" | custom-call | tf_op jit(solution)/shard_map/pallas_call | solution.py:492
  67.8 0.0 copy-done
  67.8 0.0 copy-done.1
  67.8 1.6 %bitcast_add_fusion = (f32[32,2,256]{2,1,0:T(2,128)}, f32[32,2,256]{2,1,0:T(2,128)}) fusion(f32[32,2,256]{2,1,0:T(2,128)S(1)} %copy-done, f32[2,32,2,256]{3,2,1,0:T(2,128)} %shard_map.149, f32[32,2,256]{2,1,0:T(2,128)S(1)} %copy-done.1), kind=kLoop, calls=%fused_computation | loop fusion | flops 32768 | bytes 393216 | tf_op jit(solution)/shard_map/add | solution.py:561
Async XLA Ops:
  0.6 67.2 %copy-start = (f32[32,2,256]{2,1,0:T(2,128)S(1)}, f32[32,2,256]{2,1,0:T(2,128)}, u32[]{:S(2)}) copy-start(f32[32,2,256]{2,1,0:T(2,128)} %s_hbm.1) | copy-start | bytes 196612
  0.6 67.2 %copy-start.1 = (f32[32,2,256]{2,1,0:T(2,128)S(1)}, f32[32,2,256]{2,1,0:T(2,128)}, u32[]{:S(2)}) copy-start(f32[32,2,256]{2,1,0:T(2,128)} %u_hbm.1) | copy-start | bytes 196612
